TPU v7x, 32 devices: a whole 2x2x4 slice. The times are simulated.
32 devices in a mesh: section: 4 (over z), batch: 8 (over y, x, core).
Axes of the slice: x: 2, y: 2, z: 4, core: 2. Of those that a mesh axis runs over, the one named last changes fastest.
Arguments:
- images: bfloat16 [8, 256, 1536], P('batch'), may hold values from -10 to 10
- weights: bfloat16 [4, 6, 256, 256], P('section'), may hold values from -0.375 to 0.375
- bn_mean: float32 [4, 1536], P('section'), may hold values from -3 to 3
- bn_var: float32 [4, 1536], P('section'), may hold values from 0.25 to 2
- bn_gain: float32 [4, 1536], P('section'), may hold values from 0.1 to 1.9
- bn_bias: float32 [4, 1536], P('section'), may hold values from -3 to 3
Outputs:
- image_grad: bfloat16 [8, 256, 1536], P('batch', 'section')
- loss_value: float32 [], replicated
All inputs are finite; a program needn't handle non-finite values.
Results may differ from a plain program's by a relative error of at most 0.013.
Values may be sent and summed in bfloat16 or wider, within the bound.
A program may use at most 64 MiB of HBM per device.

v0:
```python
import jax
import jax.numpy as jnp
from jax import lax
from jax.sharding import PartitionSpec as P

BLOCK = 512
MICRO = 8


EPS = 1e-05
HIGHEST = lax.Precision.HIGHEST


def from_behind(value, axis, steps):
    count = lax.axis_size(axis)
    first, last = (max(0, -steps), min(count, count - steps))
    return lax.ppermute(value, axis, [(source, source + steps) for source in range(first, last)])


def group_forward(hidden, weight):
    row_total = hidden.shape[0]
    groups, in_width, out_width = weight.shape
    pieces = hidden.reshape(row_total, groups, in_width)
    result = jnp.einsum("rgi,gio->rgo", pieces, weight, preferred_element_type=jnp.float32)
    return result.reshape(row_total, groups * out_width)


def group_backward(upstream, weight):
    row_total = upstream.shape[0]
    groups, in_width, out_width = weight.shape
    pieces = upstream.reshape(row_total, groups, out_width)
    result = jnp.einsum("rgo,gio->rgi", pieces, weight, preferred_element_type=jnp.float32)
    return result.reshape(row_total, groups * in_width)


def block_gram(pre_act, center, block_width):
    row_total, channels = pre_act.shape
    centered = (pre_act - center).reshape(row_total, channels // block_width, block_width)
    return jnp.einsum("rbi,rbj->bij", centered, centered, precision=HIGHEST)


def shards(images, weights, bn_mean, bn_var, bn_gain, bn_bias):
    sections = lax.axis_size("section")
    position = lax.axis_index("section")
    group_rows = images.shape[1]
    channels = images.shape[2]
    micro_rows = group_rows // MICRO
    block_count = channels // BLOCK
    row_total = group_rows * lax.axis_size("batch")
    weight = weights[0]
    run_mean = bn_mean[0]
    run_var = bn_var[0]
    bn_scale = bn_gain[0] * lax.rsqrt(run_var + EPS)
    bn_shift = bn_bias[0]
    source = images[0].reshape(MICRO, micro_rows, channels)
    tick_count = MICRO + sections - 1
    gram_shape = (1, 1, 1)
    stored_type = jnp.bfloat16

    def forward_tick(tick_index, loop_vars):
        incoming, stored, sum_pre, sum_gram = loop_vars
        offset_raw = tick_index - position
        in_range = (offset_raw >= 0) & (offset_raw < MICRO)
        slot_index = jnp.clip(offset_raw, 0, MICRO - 1)
        entering = lax.dynamic_index_in_dim(source, slot_index, 0, keepdims=False)
        hidden = jnp.where(position == 0, entering, incoming)

        def forward_active_step(hidden_in):
            pre_act = group_forward(hidden_in, weight)
            emitted = jax.nn.silu((pre_act - run_mean) * bn_scale + bn_shift).astype(jnp.bfloat16)
            block_sums = jnp.zeros(gram_shape, jnp.float32)
            return (pre_act, emitted, jnp.sum(pre_act, axis=0), block_sums)

        def forward_bubble_step(hidden_in):
            return (
                jnp.zeros((micro_rows, channels), jnp.float32),
                jnp.zeros((micro_rows, channels), jnp.bfloat16),
                jnp.zeros((channels,), jnp.float32),
                jnp.zeros(gram_shape, jnp.float32),
            )

        pre_act, emitted, part_sum, block_sums = lax.cond(
            in_range, forward_active_step, forward_bubble_step, hidden
        )
        previous = lax.dynamic_index_in_dim(stored, slot_index, 0, keepdims=False)
        stored = lax.dynamic_update_index_in_dim(
            stored, jnp.where(in_range, hidden, previous), slot_index, 0
        )
        incoming = from_behind(emitted, "section", 1)
        return (incoming, stored, sum_pre + part_sum, sum_gram + block_sums)

    start_vars = (
        jnp.zeros((micro_rows, channels), jnp.bfloat16),
        jnp.zeros((MICRO, micro_rows, channels), stored_type),
        jnp.zeros((channels,), jnp.float32),
        jnp.zeros(gram_shape, jnp.float32),
    )
    incoming, stored, sum_pre, sum_gram = lax.fori_loop(0, tick_count, forward_tick, start_vars)
    total_sum = lax.psum(sum_pre, "batch")
    batch_mean = total_sum / row_total
    flat_saved = stored.reshape(group_rows, channels)
    all_pre_act = group_forward(flat_saved, weight)
    covariance = lax.psum(block_gram(all_pre_act, batch_mean, BLOCK), "batch") / row_total
    var_blocks = run_var.reshape(block_count, BLOCK)
    deviation = covariance - var_blocks[:, :, None] * jnp.eye(BLOCK, dtype=jnp.float32)[None]
    layer_term = jnp.sum((batch_mean - run_mean) ** 2) + 0.25 * jnp.sum(deviation**2)
    loss_value = lax.psum(layer_term, "section") / (sections * channels)
    mean_pull = 2.0 * (batch_mean - run_mean)

    def backward_tick(tick_index, loop_vars):
        incoming, image_grads = loop_vars
        offset_raw = tick_index - (sections - 1 - position)
        in_range = (offset_raw >= 0) & (offset_raw < MICRO)
        slot_index = jnp.clip(offset_raw, 0, MICRO - 1)
        stored_item = lax.dynamic_index_in_dim(stored, slot_index, 0, keepdims=False)

        def backward_active_step(operands):
            item_in, upstream = operands
            pre_act = group_forward(item_in, weight)
            active = (pre_act - run_mean) * bn_scale + bn_shift
            sig_value = jax.nn.sigmoid(active)
            silu_slope = sig_value * (1.0 + active * (1.0 - sig_value))
            centered = (pre_act - batch_mean).reshape(micro_rows, block_count, BLOCK)
            cov_pull = jnp.einsum("rbi,bij->rbj", centered, deviation, precision=HIGHEST).reshape(
                micro_rows, channels
            )
            pre_grad = (
                upstream.astype(jnp.float32) * silu_slope * bn_scale + mean_pull + cov_pull
            ).astype(jnp.bfloat16)
            return group_backward(pre_grad, weight).astype(jnp.bfloat16)

        def backward_bubble_step(operands):
            return jnp.zeros((micro_rows, channels), jnp.bfloat16)

        sent_back = lax.cond(
            in_range, backward_active_step, backward_bubble_step, (stored_item, incoming)
        )
        previous = lax.dynamic_index_in_dim(image_grads, slot_index, 0, keepdims=False)
        image_grads = lax.dynamic_update_index_in_dim(
            image_grads, jnp.where(in_range, sent_back, previous), slot_index, 0
        )
        incoming = from_behind(sent_back, "section", -1)
        return (incoming, image_grads)

    back_vars = (
        jnp.zeros((micro_rows, channels), jnp.bfloat16),
        jnp.zeros((MICRO, micro_rows, channels), jnp.bfloat16),
    )
    incoming, image_grads = lax.fori_loop(0, tick_count, backward_tick, back_vars)
    flat_grads = image_grads.reshape(group_rows, channels)
    own_term = jnp.where(
        position == 0,
        flat_grads.astype(jnp.float32),
        jnp.zeros((group_rows, channels), jnp.float32),
    )
    own_rows = lax.psum_scatter(
        own_term.astype(jnp.bfloat16), "section", scatter_dimension=0, tiled=True
    )
    return (own_rows[None], loss_value)


def solution(mesh):
    placed = (
        P("batch", None, None),
        P("section", None, None, None),
        P("section", None),
        P("section", None),
        P("section", None),
        P("section", None),
    )
    return jax.shard_map(
        shards,
        mesh=mesh,
        in_specs=placed,
        out_specs=(P("batch", "section", None), P()),
        check_vma=False,
    )
```

profile of v0, /device:TPU:0, one launch (start us, length us, event | category | flops | bytes accessed | tf_op | source)
XLA Modules:
  0.0 372.0 jit_solution(11636706364624408886)
XLA Ops:
  8.1 108.2 %while.37 = (s32[]{:T(128)}, bf16[32,1536]{1,0:T(8,128)(2,1)S(1)}, bf16[8,32,1536]{2,1,0:T(8,128)(2,1)S(1)}, f32[1536]{0:T(1024)S(1)}, s32[]{:T(128)}, /*index=5...) while((s32[]{:T(128)}, bf16[32,1536]{1,0:T(8,128)(2,1)S(1)}, ...), condition=%wide.region_4.5_spmd.clone, body=%wide.region_0.4_spmd.clone.sunk | while | flops 25708040 | bytes 2931015 | solution.py:98
  9.1 3.0 conditional.6
  14.1 2.2 collective-permute-done.1
  17.2 3.0 conditional.6
  20.2 4.4 %collective-permute-start.1 = (bf16[32,1536]{1,0:T(8,128)(2,1)S(1)}, bf16[32,1536]{1,0:T(8,128)(2,1)S(1)}, u32[]{:S(2)}, u32[]{:S(2)}) collective-permute-start(bf16[32,1536]{1,0:T(8,128)(2,1)S(1)} %get-tuple-element.814), channel_id=1, source_target_pairs={{0,8},{8,16},{16,24},{1,9},{9,17},{17,25},{2,10},{10,18},{18,26},{... | collective-permute-start | bytes 294920 | tf_op jit(solution)/shard_map/while/body/eval_jaxpr/ppermute | solution.py:17
  24.6 2.2 collective-permute-done.1
  27.7 3.0 conditional.6
  30.7 4.3 %collective-permute-start.1 = (bf16[32,1536]{1,0:T(8,128)(2,1)S(1)}, bf16[32,1536]{1,0:T(8,128)(2,1)S(1)}, u32[]{:S(2)}, u32[]{:S(2)}) collective-permute-start(bf16[32,1536]{1,0:T(8,128)(2,1)S(1)} %get-tuple-element.814), channel_id=1, source_target_pairs={{0,8},{8,16},{16,24},{1,9},{9,17},{17,25},{2,10},{10,18},{18,26},{... | collective-permute-start | bytes 294920 | tf_op jit(solution)/shard_map/while/body/eval_jaxpr/ppermute | solution.py:17
  35.0 2.2 collective-permute-done.1
  38.1 3.0 conditional.6
  41.1 4.3 %collective-permute-start.1 = (bf16[32,1536]{1,0:T(8,128)(2,1)S(1)}, bf16[32,1536]{1,0:T(8,128)(2,1)S(1)}, u32[]{:S(2)}, u32[]{:S(2)}) collective-permute-start(bf16[32,1536]{1,0:T(8,128)(2,1)S(1)} %get-tuple-element.814), channel_id=1, source_target_pairs={{0,8},{8,16},{16,24},{1,9},{9,17},{17,25},{2,10},{10,18},{18,26},{... | collective-permute-start | bytes 294920 | tf_op jit(solution)/shard_map/while/body/eval_jaxpr/ppermute | solution.py:17
  45.4 2.2 collective-permute-done.1
  48.6 3.0 conditional.6
  51.5 4.3 %collective-permute-start.1 = (bf16[32,1536]{1,0:T(8,128)(2,1)S(1)}, bf16[32,1536]{1,0:T(8,128)(2,1)S(1)}, u32[]{:S(2)}, u32[]{:S(2)}) collective-permute-start(bf16[32,1536]{1,0:T(8,128)(2,1)S(1)} %get-tuple-element.814), channel_id=1, source_target_pairs={{0,8},{8,16},{16,24},{1,9},{9,17},{17,25},{2,10},{10,18},{18,26},{... | collective-permute-start | bytes 294920 | tf_op jit(solution)/shard_map/while/body/eval_jaxpr/ppermute | solution.py:17
  55.9 2.2 collective-permute-done.1
  59.0 3.0 conditional.6
  61.9 4.3 %collective-permute-start.1 = (bf16[32,1536]{1,0:T(8,128)(2,1)S(1)}, bf16[32,1536]{1,0:T(8,128)(2,1)S(1)}, u32[]{:S(2)}, u32[]{:S(2)}) collective-permute-start(bf16[32,1536]{1,0:T(8,128)(2,1)S(1)} %get-tuple-element.814), channel_id=1, source_target_pairs={{0,8},{8,16},{16,24},{1,9},{9,17},{17,25},{2,10},{10,18},{18,26},{... | collective-permute-start | bytes 294920 | tf_op jit(solution)/shard_map/while/body/eval_jaxpr/ppermute | solution.py:17
  66.3 2.2 collective-permute-done.1
  69.4 3.0 conditional.6
  72.4 4.3 %collective-permute-start.1 = (bf16[32,1536]{1,0:T(8,128)(2,1)S(1)}, bf16[32,1536]{1,0:T(8,128)(2,1)S(1)}, u32[]{:S(2)}, u32[]{:S(2)}) collective-permute-start(bf16[32,1536]{1,0:T(8,128)(2,1)S(1)} %get-tuple-element.814), channel_id=1, source_target_pairs={{0,8},{8,16},{16,24},{1,9},{9,17},{17,25},{2,10},{10,18},{18,26},{... | collective-permute-start | bytes 294920 | tf_op jit(solution)/shard_map/while/body/eval_jaxpr/ppermute | solution.py:17
  76.7 2.2 collective-permute-done.1
  79.8 3.0 conditional.6
  82.8 4.3 %collective-permute-start.1 = (bf16[32,1536]{1,0:T(8,128)(2,1)S(1)}, bf16[32,1536]{1,0:T(8,128)(2,1)S(1)}, u32[]{:S(2)}, u32[]{:S(2)}) collective-permute-start(bf16[32,1536]{1,0:T(8,128)(2,1)S(1)} %get-tuple-element.814), channel_id=1, source_target_pairs={{0,8},{8,16},{16,24},{1,9},{9,17},{17,25},{2,10},{10,18},{18,26},{... | collective-permute-start | bytes 294920 | tf_op jit(solution)/shard_map/while/body/eval_jaxpr/ppermute | solution.py:17
  87.1 2.6 collective-permute-done.1
  90.8 7.3 %collective-permute-start.1 = (bf16[32,1536]{1,0:T(8,128)(2,1)S(1)}, bf16[32,1536]{1,0:T(8,128)(2,1)S(1)}, u32[]{:S(2)}, u32[]{:S(2)}) collective-permute-start(bf16[32,1536]{1,0:T(8,128)(2,1)S(1)} %get-tuple-element.814), channel_id=1, source_target_pairs={{0,8},{8,16},{16,24},{1,9},{9,17},{17,25},{2,10},{10,18},{18,26},{... | collective-permute-start | bytes 294920 | tf_op jit(solution)/shard_map/while/body/eval_jaxpr/ppermute | solution.py:17
  98.1 2.2 collective-permute-done.1
  101.3 4.3 %collective-permute-start.1 = (bf16[32,1536]{1,0:T(8,128)(2,1)S(1)}, bf16[32,1536]{1,0:T(8,128)(2,1)S(1)}, u32[]{:S(2)}, u32[]{:S(2)}) collective-permute-start(bf16[32,1536]{1,0:T(8,128)(2,1)S(1)} %get-tuple-element.814), channel_id=1, source_target_pairs={{0,8},{8,16},{16,24},{1,9},{9,17},{17,25},{2,10},{10,18},{18,26},{... | collective-permute-start | bytes 294920 | tf_op jit(solution)/shard_map/while/body/eval_jaxpr/ppermute | solution.py:17
  105.7 2.2 collective-permute-done.1
  108.8 5.2 %collective-permute-start.1 = (bf16[32,1536]{1,0:T(8,128)(2,1)S(1)}, bf16[32,1536]{1,0:T(8,128)(2,1)S(1)}, u32[]{:S(2)}, u32[]{:S(2)}) collective-permute-start(bf16[32,1536]{1,0:T(8,128)(2,1)S(1)} %get-tuple-element.814), channel_id=1, source_target_pairs={{0,8},{8,16},{16,24},{1,9},{9,17},{17,25},{2,10},{10,18},{18,26},{... | collective-permute-start | bytes 294920 | tf_op jit(solution)/shard_map/while/body/eval_jaxpr/ppermute | solution.py:17
  114.1 2.2 collective-permute-done.1
  116.2 12.2 %psum.21 = f32[1536]{0:T(1024)S(1)} all-reduce(f32[1536]{0:T(1024)S(1)} %get-tuple-element.572), channel_id=1, replica_groups=mesh['section'=4,'batch'=8] {'batch'}, use_global_device_ids=true, to_apply=%region_5.6 | all-reduce | flops 1536 | bytes 12288 | tf_op jit(solution)/shard_map/psum | solution.py:99
  132.3 4.5 %fusion.9 = f32[3,512,512]{2,1,0:T(8,128)} fusion(f32[256,3,512]{0,2,1:T(8,128)S(1)} %bitcast.72, f32[3,512]{1,0:T(4,128)S(1)} %sub.85), kind=kOutput, calls=%fused_computation.27 | convolution fusion | flops 2416312320 | bytes 4724736 | tf_op jit(solution)/shard_map/rbi,rbj->bij/dot_general | solution.py:39
  137.1 73.7 %all-reduce.2.cloned.1.call-done = f32[3,512,512]{2,1,0:T(8,128)} async-done(((f32[3,512,512]{2,1,0:T(8,128)}), f32[3,512,512]{2,1,0:T(8,128)}) %all-reduce.2.cloned.1.call-update) | async-done | bytes 3145744 | tf_op jit(solution)/shard_map/psum | solution.py:103
  210.7 4.6 %multiply_reduce_fusion = (f32[]{:T(128)}, f32[3,512,512]{2,1,0:T(8,128)}) fusion(f32[512,512]{1,0:T(8,128)S(1)} %fusion.11, f32[3,512]{1,0:T(4,128)S(1)} %mul.72, f32[3,512,512]{2,1,0:T(8,128)} %all-reduce.2.cloned.1.call-done), kind=kLoop, calls=%fused_computation.24 | loop fusion | flops 3932159 | bytes 7346180 | tf_op jit(solution)/shard_map/reduce_sum | solution.py:106
  215.5 126.5 %while.36 = (s32[]{:T(128)}, bf16[32,1536]{1,0:T(8,128)(2,1)S(1)}, bf16[8,32,1536]{2,1,0:T(8,128)(2,1)S(1)}, s32[]{:T(128)}, bf16[8,32,1536]{2,1,0:T(8,128)(2,1)...) while((s32[]{:T(128)}, bf16[32,1536]{1,0:T(8,128)(2,1)S(1)}, ...), condition=%wide.region_10.11_spmd, body=%wide.region_7.10_spmd.sunk | while | flops 353255424 | bytes 9701736 | solution.py:149
  216.9 5.1 %collective-permute-done = bf16[32,1536]{1,0:T(8,128)(2,1)S(1)} collective-permute-done((bf16[32,1536]{1,0:T(8,128)(2,1)S(1)}, bf16[32,1536]{1,0:T(8,128)(2,1)S(1)}, u32[]{:S(2)}, u32[]{:S(2)}) %collective-permute-start) | collective-permute-done | bytes 98336 | tf_op jit(solution)/shard_map/while/body/eval_jaxpr/ppermute | solution.py:17
  223.5 5.1 %collective-permute-done = bf16[32,1536]{1,0:T(8,128)(2,1)S(1)} collective-permute-done((bf16[32,1536]{1,0:T(8,128)(2,1)S(1)}, bf16[32,1536]{1,0:T(8,128)(2,1)S(1)}, u32[]{:S(2)}, u32[]{:S(2)}) %collective-permute-start) | collective-permute-done | bytes 98336 | tf_op jit(solution)/shard_map/while/body/eval_jaxpr/ppermute | solution.py:17
  230.0 18.2 %collective-permute-done = bf16[32,1536]{1,0:T(8,128)(2,1)S(1)} collective-permute-done((bf16[32,1536]{1,0:T(8,128)(2,1)S(1)}, bf16[32,1536]{1,0:T(8,128)(2,1)S(1)}, u32[]{:S(2)}, u32[]{:S(2)}) %collective-permute-start) | collective-permute-done | bytes 98336 | tf_op jit(solution)/shard_map/while/body/eval_jaxpr/ppermute | solution.py:17
  248.2 5.1 %conditional.5 = (bf16[32,1536]{1,0:T(8,128)(2,1)S(1)}) conditional(s32[]{:T(128)} %convert_element_type.71, () %tuple.98, (bf16[32,1536]{1,0:T(8,128)(2,1)S(1)}, bf16[8,32,1536]{2,1,0:T(8,128)(2,1)S(1)}, s32[]{:T(128)}, bf16[6,256,256]{2,1,0:T(8,128)(2,1)S(1)}, f32[1,1536]{1,0:T(1,128)S(1)}, /*index=5*/f32[1536]{0:T(1024)S(1)}, ...), branch_computations={%region_8.8_spmd, %region_9.9_spmd} | conditional | flops 353206272 | bytes 8816660 | solution.py:135
  248.9 3.8 %convolution_bitcast_fusion = f32[3,4,8,512]{3,2,1,0:T(8,128)S(1)} fusion(f32[3,512,512]{2,1,0:T(8,128)} %get-tuple-element.552, f32[32,3,512]{2,1,0:T(4,128)S(1)} %broadcast_subtract_fusion), kind=kOutput, calls=%fused_computation.10 | convolution fusion | flops 301989888 | bytes 3538944 | tf_op jit(solution)/shard_map/while/body/eval_jaxpr/cond/branch_1_fun/rbi,bij->rbj/dot_general | solution.py:124
  254.7 5.1 %collective-permute-done = bf16[32,1536]{1,0:T(8,128)(2,1)S(1)} collective-permute-done((bf16[32,1536]{1,0:T(8,128)(2,1)S(1)}, bf16[32,1536]{1,0:T(8,128)(2,1)S(1)}, u32[]{:S(2)}, u32[]{:S(2)}) %collective-permute-start) | collective-permute-done | bytes 98336 | tf_op jit(solution)/shard_map/while/body/eval_jaxpr/ppermute | solution.py:17
  259.8 5.1 %conditional.5 = (bf16[32,1536]{1,0:T(8,128)(2,1)S(1)}) conditional(s32[]{:T(128)} %convert_element_type.71, () %tuple.98, (bf16[32,1536]{1,0:T(8,128)(2,1)S(1)}, bf16[8,32,1536]{2,1,0:T(8,128)(2,1)S(1)}, s32[]{:T(128)}, bf16[6,256,256]{2,1,0:T(8,128)(2,1)S(1)}, f32[1,1536]{1,0:T(1,128)S(1)}, /*index=5*/f32[1536]{0:T(1024)S(1)}, ...), branch_computations={%region_8.8_spmd, %region_9.9_spmd} | conditional | flops 353206272 | bytes 8816660 | solution.py:135
  260.5 3.8 %convolution_bitcast_fusion = f32[3,4,8,512]{3,2,1,0:T(8,128)S(1)} fusion(f32[3,512,512]{2,1,0:T(8,128)} %get-tuple-element.552, f32[32,3,512]{2,1,0:T(4,128)S(1)} %broadcast_subtract_fusion), kind=kOutput, calls=%fused_computation.10 | convolution fusion | flops 301989888 | bytes 3538944 | tf_op jit(solution)/shard_map/while/body/eval_jaxpr/cond/branch_1_fun/rbi,bij->rbj/dot_general | solution.py:124
  266.3 5.1 %collective-permute-done = bf16[32,1536]{1,0:T(8,128)(2,1)S(1)} collective-permute-done((bf16[32,1536]{1,0:T(8,128)(2,1)S(1)}, bf16[32,1536]{1,0:T(8,128)(2,1)S(1)}, u32[]{:S(2)}, u32[]{:S(2)}) %collective-permute-start) | collective-permute-done | bytes 98336 | tf_op jit(solution)/shard_map/while/body/eval_jaxpr/ppermute | solution.py:17
  271.4 5.1 %conditional.5 = (bf16[32,1536]{1,0:T(8,128)(2,1)S(1)}) conditional(s32[]{:T(128)} %convert_element_type.71, () %tuple.98, (bf16[32,1536]{1,0:T(8,128)(2,1)S(1)}, bf16[8,32,1536]{2,1,0:T(8,128)(2,1)S(1)}, s32[]{:T(128)}, bf16[6,256,256]{2,1,0:T(8,128)(2,1)S(1)}, f32[1,1536]{1,0:T(1,128)S(1)}, /*index=5*/f32[1536]{0:T(1024)S(1)}, ...), branch_computations={%region_8.8_spmd, %region_9.9_spmd} | conditional | flops 353206272 | bytes 8816660 | solution.py:135
  272.1 3.8 %convolution_bitcast_fusion = f32[3,4,8,512]{3,2,1,0:T(8,128)S(1)} fusion(f32[3,512,512]{2,1,0:T(8,128)} %get-tuple-element.552, f32[32,3,512]{2,1,0:T(4,128)S(1)} %broadcast_subtract_fusion), kind=kOutput, calls=%fused_computation.10 | convolution fusion | flops 301989888 | bytes 3538944 | tf_op jit(solution)/shard_map/while/body/eval_jaxpr/cond/branch_1_fun/rbi,bij->rbj/dot_general | solution.py:124
  277.9 5.1 %collective-permute-done = bf16[32,1536]{1,0:T(8,128)(2,1)S(1)} collective-permute-done((bf16[32,1536]{1,0:T(8,128)(2,1)S(1)}, bf16[32,1536]{1,0:T(8,128)(2,1)S(1)}, u32[]{:S(2)}, u32[]{:S(2)}) %collective-permute-start) | collective-permute-done | bytes 98336 | tf_op jit(solution)/shard_map/while/body/eval_jaxpr/ppermute | solution.py:17
  283.0 5.1 %conditional.5 = (bf16[32,1536]{1,0:T(8,128)(2,1)S(1)}) conditional(s32[]{:T(128)} %convert_element_type.71, () %tuple.98, (bf16[32,1536]{1,0:T(8,128)(2,1)S(1)}, bf16[8,32,1536]{2,1,0:T(8,128)(2,1)S(1)}, s32[]{:T(128)}, bf16[6,256,256]{2,1,0:T(8,128)(2,1)S(1)}, f32[1,1536]{1,0:T(1,128)S(1)}, /*index=5*/f32[1536]{0:T(1024)S(1)}, ...), branch_computations={%region_8.8_spmd, %region_9.9_spmd} | conditional | flops 353206272 | bytes 8816660 | solution.py:135
  283.7 3.8 %convolution_bitcast_fusion = f32[3,4,8,512]{3,2,1,0:T(8,128)S(1)} fusion(f32[3,512,512]{2,1,0:T(8,128)} %get-tuple-element.552, f32[32,3,512]{2,1,0:T(4,128)S(1)} %broadcast_subtract_fusion), kind=kOutput, calls=%fused_computation.10 | convolution fusion | flops 301989888 | bytes 3538944 | tf_op jit(solution)/shard_map/while/body/eval_jaxpr/cond/branch_1_fun/rbi,bij->rbj/dot_general | solution.py:124
  289.5 5.1 %collective-permute-done = bf16[32,1536]{1,0:T(8,128)(2,1)S(1)} collective-permute-done((bf16[32,1536]{1,0:T(8,128)(2,1)S(1)}, bf16[32,1536]{1,0:T(8,128)(2,1)S(1)}, u32[]{:S(2)}, u32[]{:S(2)}) %collective-permute-start) | collective-permute-done | bytes 98336 | tf_op jit(solution)/shard_map/while/body/eval_jaxpr/ppermute | solution.py:17
  294.6 5.1 %conditional.5 = (bf16[32,1536]{1,0:T(8,128)(2,1)S(1)}) conditional(s32[]{:T(128)} %convert_element_type.71, () %tuple.98, (bf16[32,1536]{1,0:T(8,128)(2,1)S(1)}, bf16[8,32,1536]{2,1,0:T(8,128)(2,1)S(1)}, s32[]{:T(128)}, bf16[6,256,256]{2,1,0:T(8,128)(2,1)S(1)}, f32[1,1536]{1,0:T(1,128)S(1)}, /*index=5*/f32[1536]{0:T(1024)S(1)}, ...), branch_computations={%region_8.8_spmd, %region_9.9_spmd} | conditional | flops 353206272 | bytes 8816660 | solution.py:135
  295.3 3.8 %convolution_bitcast_fusion = f32[3,4,8,512]{3,2,1,0:T(8,128)S(1)} fusion(f32[3,512,512]{2,1,0:T(8,128)} %get-tuple-element.552, f32[32,3,512]{2,1,0:T(4,128)S(1)} %broadcast_subtract_fusion), kind=kOutput, calls=%fused_computation.10 | convolution fusion | flops 301989888 | bytes 3538944 | tf_op jit(solution)/shard_map/while/body/eval_jaxpr/cond/branch_1_fun/rbi,bij->rbj/dot_general | solution.py:124
  301.1 5.1 %collective-permute-done = bf16[32,1536]{1,0:T(8,128)(2,1)S(1)} collective-permute-done((bf16[32,1536]{1,0:T(8,128)(2,1)S(1)}, bf16[32,1536]{1,0:T(8,128)(2,1)S(1)}, u32[]{:S(2)}, u32[]{:S(2)}) %collective-permute-start) | collective-permute-done | bytes 98336 | tf_op jit(solution)/shard_map/while/body/eval_jaxpr/ppermute | solution.py:17
  306.3 5.1 %conditional.5 = (bf16[32,1536]{1,0:T(8,128)(2,1)S(1)}) conditional(s32[]{:T(128)} %convert_element_type.71, () %tuple.98, (bf16[32,1536]{1,0:T(8,128)(2,1)S(1)}, bf16[8,32,1536]{2,1,0:T(8,128)(2,1)S(1)}, s32[]{:T(128)}, bf16[6,256,256]{2,1,0:T(8,128)(2,1)S(1)}, f32[1,1536]{1,0:T(1,128)S(1)}, /*index=5*/f32[1536]{0:T(1024)S(1)}, ...), branch_computations={%region_8.8_spmd, %region_9.9_spmd} | conditional | flops 353206272 | bytes 8816660 | solution.py:135
  307.0 3.8 %convolution_bitcast_fusion = f32[3,4,8,512]{3,2,1,0:T(8,128)S(1)} fusion(f32[3,512,512]{2,1,0:T(8,128)} %get-tuple-element.552, f32[32,3,512]{2,1,0:T(4,128)S(1)} %broadcast_subtract_fusion), kind=kOutput, calls=%fused_computation.10 | convolution fusion | flops 301989888 | bytes 3538944 | tf_op jit(solution)/shard_map/while/body/eval_jaxpr/cond/branch_1_fun/rbi,bij->rbj/dot_general | solution.py:124
  312.7 5.5 %collective-permute-done = bf16[32,1536]{1,0:T(8,128)(2,1)S(1)} collective-permute-done((bf16[32,1536]{1,0:T(8,128)(2,1)S(1)}, bf16[32,1536]{1,0:T(8,128)(2,1)S(1)}, u32[]{:S(2)}, u32[]{:S(2)}) %collective-permute-start) | collective-permute-done | bytes 98336 | tf_op jit(solution)/shard_map/while/body/eval_jaxpr/ppermute | solution.py:17
  318.2 5.1 %conditional.5 = (bf16[32,1536]{1,0:T(8,128)(2,1)S(1)}) conditional(s32[]{:T(128)} %convert_element_type.71, () %tuple.98, (bf16[32,1536]{1,0:T(8,128)(2,1)S(1)}, bf16[8,32,1536]{2,1,0:T(8,128)(2,1)S(1)}, s32[]{:T(128)}, bf16[6,256,256]{2,1,0:T(8,128)(2,1)S(1)}, f32[1,1536]{1,0:T(1,128)S(1)}, /*index=5*/f32[1536]{0:T(1024)S(1)}, ...), branch_computations={%region_8.8_spmd, %region_9.9_spmd} | conditional | flops 353206272 | bytes 8816660 | solution.py:135
  318.9 3.8 %convolution_bitcast_fusion = f32[3,4,8,512]{3,2,1,0:T(8,128)S(1)} fusion(f32[3,512,512]{2,1,0:T(8,128)} %get-tuple-element.552, f32[32,3,512]{2,1,0:T(4,128)S(1)} %broadcast_subtract_fusion), kind=kOutput, calls=%fused_computation.10 | convolution fusion | flops 301989888 | bytes 3538944 | tf_op jit(solution)/shard_map/while/body/eval_jaxpr/cond/branch_1_fun/rbi,bij->rbj/dot_general | solution.py:124
  324.7 5.8 %collective-permute-done = bf16[32,1536]{1,0:T(8,128)(2,1)S(1)} collective-permute-done((bf16[32,1536]{1,0:T(8,128)(2,1)S(1)}, bf16[32,1536]{1,0:T(8,128)(2,1)S(1)}, u32[]{:S(2)}, u32[]{:S(2)}) %collective-permute-start) | collective-permute-done | bytes 98336 | tf_op jit(solution)/shard_map/while/body/eval_jaxpr/ppermute | solution.py:17
  330.4 5.1 %conditional.5 = (bf16[32,1536]{1,0:T(8,128)(2,1)S(1)}) conditional(s32[]{:T(128)} %convert_element_type.71, () %tuple.98, (bf16[32,1536]{1,0:T(8,128)(2,1)S(1)}, bf16[8,32,1536]{2,1,0:T(8,128)(2,1)S(1)}, s32[]{:T(128)}, bf16[6,256,256]{2,1,0:T(8,128)(2,1)S(1)}, f32[1,1536]{1,0:T(1,128)S(1)}, /*index=5*/f32[1536]{0:T(1024)S(1)}, ...), branch_computations={%region_8.8_spmd, %region_9.9_spmd} | conditional | flops 353206272 | bytes 8816660 | solution.py:135
  331.1 3.8 %convolution_bitcast_fusion = f32[3,4,8,512]{3,2,1,0:T(8,128)S(1)} fusion(f32[3,512,512]{2,1,0:T(8,128)} %get-tuple-element.552, f32[32,3,512]{2,1,0:T(4,128)S(1)} %broadcast_subtract_fusion), kind=kOutput, calls=%fused_computation.10 | convolution fusion | flops 301989888 | bytes 3538944 | tf_op jit(solution)/shard_map/while/body/eval_jaxpr/cond/branch_1_fun/rbi,bij->rbj/dot_general | solution.py:124
  336.9 5.1 %collective-permute-done = bf16[32,1536]{1,0:T(8,128)(2,1)S(1)} collective-permute-done((bf16[32,1536]{1,0:T(8,128)(2,1)S(1)}, bf16[32,1536]{1,0:T(8,128)(2,1)S(1)}, u32[]{:S(2)}, u32[]{:S(2)}) %collective-permute-start) | collective-permute-done | bytes 98336 | tf_op jit(solution)/shard_map/while/body/eval_jaxpr/ppermute | solution.py:17
  344.4 9.0 %psum.23 = f32[]{:T(128)} all-reduce(f32[]{:T(128)S(6)} %add.126), channel_id=1, replica_groups=mesh['section'=4,'batch'=8] {'section'}, use_global_device_ids=true, to_apply=%region_14.15 | all-reduce | flops 1 | bytes 8 | tf_op jit(solution)/shard_map/psum | solution.py:107
  354.0 10.1 %reduce-scatter.2.cloned.1.call-done = bf16[64,1536]{1,0:T(8,128)(2,1)} async-done(((bf16[256,1536]{1,0:T(8,128)(2,1)}), bf16[64,1536]{1,0:T(8,128)(2,1)}) %reduce-scatter.2.cloned.1.call-update) | async-done | bytes 196624 | tf_op jit(solution)/shard_map/reduce_scatter | solution.py:156
  (266 shorter events, 66.2 us)
Async XLA Ops:
  7.2 203.6 %all-reduce.2.cloned.1.call-start = ((), (), s32[]{:S(2)}) async-start(), calls=%async_computation.1 | async-start | bytes 6291456 | tf_op jit(solution)/shard_map/psum | solution.py:103
  12.0 4.2 %collective-permute-start.1 = (bf16[32,1536]{1,0:T(8,128)(2,1)S(1)}, bf16[32,1536]{1,0:T(8,128)(2,1)S(1)}, u32[]{:S(2)}, u32[]{:S(2)}) collective-permute-start(bf16[32,1536]{1,0:T(8,128)(2,1)S(1)} %get-tuple-element.814), channel_id=1, source_target_pairs={{0,8},{8,16},{16,24},{1,9},{9,17},{17,25},{2,10},{10,18},{18,26},{... | collective-permute-start | bytes 294920 | tf_op jit(solution)/shard_map/while/body/eval_jaxpr/ppermute | solution.py:17
  20.2 6.6 %collective-permute-start.1 = (bf16[32,1536]{1,0:T(8,128)(2,1)S(1)}, bf16[32,1536]{1,0:T(8,128)(2,1)S(1)}, u32[]{:S(2)}, u32[]{:S(2)}) collective-permute-start(bf16[32,1536]{1,0:T(8,128)(2,1)S(1)} %get-tuple-element.814), channel_id=1, source_target_pairs={{0,8},{8,16},{16,24},{1,9},{9,17},{17,25},{2,10},{10,18},{18,26},{... | collective-permute-start | bytes 294920 | tf_op jit(solution)/shard_map/while/body/eval_jaxpr/ppermute | solution.py:17
  30.7 6.5 %collective-permute-start.1 = (bf16[32,1536]{1,0:T(8,128)(2,1)S(1)}, bf16[32,1536]{1,0:T(8,128)(2,1)S(1)}, u32[]{:S(2)}, u32[]{:S(2)}) collective-permute-start(bf16[32,1536]{1,0:T(8,128)(2,1)S(1)} %get-tuple-element.814), channel_id=1, source_target_pairs={{0,8},{8,16},{16,24},{1,9},{9,17},{17,25},{2,10},{10,18},{18,26},{... | collective-permute-start | bytes 294920 | tf_op jit(solution)/shard_map/while/body/eval_jaxpr/ppermute | solution.py:17
  41.1 6.5 %collective-permute-start.1 = (bf16[32,1536]{1,0:T(8,128)(2,1)S(1)}, bf16[32,1536]{1,0:T(8,128)(2,1)S(1)}, u32[]{:S(2)}, u32[]{:S(2)}) collective-permute-start(bf16[32,1536]{1,0:T(8,128)(2,1)S(1)} %get-tuple-element.814), channel_id=1, source_target_pairs={{0,8},{8,16},{16,24},{1,9},{9,17},{17,25},{2,10},{10,18},{18,26},{... | collective-permute-start | bytes 294920 | tf_op jit(solution)/shard_map/while/body/eval_jaxpr/ppermute | solution.py:17
  51.5 6.5 %collective-permute-start.1 = (bf16[32,1536]{1,0:T(8,128)(2,1)S(1)}, bf16[32,1536]{1,0:T(8,128)(2,1)S(1)}, u32[]{:S(2)}, u32[]{:S(2)}) collective-permute-start(bf16[32,1536]{1,0:T(8,128)(2,1)S(1)} %get-tuple-element.814), channel_id=1, source_target_pairs={{0,8},{8,16},{16,24},{1,9},{9,17},{17,25},{2,10},{10,18},{18,26},{... | collective-permute-start | bytes 294920 | tf_op jit(solution)/shard_map/while/body/eval_jaxpr/ppermute | solution.py:17
  61.9 6.5 %collective-permute-start.1 = (bf16[32,1536]{1,0:T(8,128)(2,1)S(1)}, bf16[32,1536]{1,0:T(8,128)(2,1)S(1)}, u32[]{:S(2)}, u32[]{:S(2)}) collective-permute-start(bf16[32,1536]{1,0:T(8,128)(2,1)S(1)} %get-tuple-element.814), channel_id=1, source_target_pairs={{0,8},{8,16},{16,24},{1,9},{9,17},{17,25},{2,10},{10,18},{18,26},{... | collective-permute-start | bytes 294920 | tf_op jit(solution)/shard_map/while/body/eval_jaxpr/ppermute | solution.py:17
  72.4 6.5 %collective-permute-start.1 = (bf16[32,1536]{1,0:T(8,128)(2,1)S(1)}, bf16[32,1536]{1,0:T(8,128)(2,1)S(1)}, u32[]{:S(2)}, u32[]{:S(2)}) collective-permute-start(bf16[32,1536]{1,0:T(8,128)(2,1)S(1)} %get-tuple-element.814), channel_id=1, source_target_pairs={{0,8},{8,16},{16,24},{1,9},{9,17},{17,25},{2,10},{10,18},{18,26},{... | collective-permute-start | bytes 294920 | tf_op jit(solution)/shard_map/while/body/eval_jaxpr/ppermute | solution.py:17
  82.8 7.0 %collective-permute-start.1 = (bf16[32,1536]{1,0:T(8,128)(2,1)S(1)}, bf16[32,1536]{1,0:T(8,128)(2,1)S(1)}, u32[]{:S(2)}, u32[]{:S(2)}) collective-permute-start(bf16[32,1536]{1,0:T(8,128)(2,1)S(1)} %get-tuple-element.814), channel_id=1, source_target_pairs={{0,8},{8,16},{16,24},{1,9},{9,17},{17,25},{2,10},{10,18},{18,26},{... | collective-permute-start | bytes 294920 | tf_op jit(solution)/shard_map/while/body/eval_jaxpr/ppermute | solution.py:17
  90.8 9.5 %collective-permute-start.1 = (bf16[32,1536]{1,0:T(8,128)(2,1)S(1)}, bf16[32,1536]{1,0:T(8,128)(2,1)S(1)}, u32[]{:S(2)}, u32[]{:S(2)}) collective-permute-start(bf16[32,1536]{1,0:T(8,128)(2,1)S(1)} %get-tuple-element.814), channel_id=1, source_target_pairs={{0,8},{8,16},{16,24},{1,9},{9,17},{17,25},{2,10},{10,18},{18,26},{... | collective-permute-start | bytes 294920 | tf_op jit(solution)/shard_map/while/body/eval_jaxpr/ppermute | solution.py:17
  101.3 6.5 %collective-permute-start.1 = (bf16[32,1536]{1,0:T(8,128)(2,1)S(1)}, bf16[32,1536]{1,0:T(8,128)(2,1)S(1)}, u32[]{:S(2)}, u32[]{:S(2)}) collective-permute-start(bf16[32,1536]{1,0:T(8,128)(2,1)S(1)} %get-tuple-element.814), channel_id=1, source_target_pairs={{0,8},{8,16},{16,24},{1,9},{9,17},{17,25},{2,10},{10,18},{18,26},{... | collective-permute-start | bytes 294920 | tf_op jit(solution)/shard_map/while/body/eval_jaxpr/ppermute | solution.py:17
  108.8 7.4 %collective-permute-start.1 = (bf16[32,1536]{1,0:T(8,128)(2,1)S(1)}, bf16[32,1536]{1,0:T(8,128)(2,1)S(1)}, u32[]{:S(2)}, u32[]{:S(2)}) collective-permute-start(bf16[32,1536]{1,0:T(8,128)(2,1)S(1)} %get-tuple-element.814), channel_id=1, source_target_pairs={{0,8},{8,16},{16,24},{1,9},{9,17},{17,25},{2,10},{10,18},{18,26},{... | collective-permute-start | bytes 294920 | tf_op jit(solution)/shard_map/while/body/eval_jaxpr/ppermute | solution.py:17
  136.8 227.2 %reduce-scatter.2.cloned.1.call-start = ((), (), s32[]{:S(2)}) async-start(), calls=%async_computation.2 | async-start | bytes 983040 | tf_op jit(solution)/shard_map/reduce_scatter | solution.py:156
  137.0 78.5 %copy-start = (bf16[6,256,256]{2,1,0:T(8,128)(2,1)S(1)}, bf16[6,256,256]{2,1,0:T(8,128)(2,1)}, u32[]{:S(2)}) copy-start(bf16[6,256,256]{2,1,0:T(8,128)(2,1)} %get-tuple-element.917) | copy-start | bytes 2359300
  137.0 78.5 %copy-start.1 = (f32[1,1536]{1,0:T(1,128)S(1)}, f32[1,1536]{1,0:T(1,128)}, u32[]{:S(2)}) copy-start(f32[1,1536]{1,0:T(1,128)} %get-tuple-element.928) | copy-start | bytes 18436
  137.0 78.5 %copy-start.2 = (f32[1,1536]{1,0:T(1,128)S(1)}, f32[1,1536]{1,0:T(1,128)}, u32[]{:S(2)}) copy-start(f32[1,1536]{1,0:T(1,128)} %get-tuple-element.929) | copy-start | bytes 18436
  215.6 6.5 %collective-permute-start = (bf16[32,1536]{1,0:T(8,128)(2,1)S(1)}, bf16[32,1536]{1,0:T(8,128)(2,1)S(1)}, u32[]{:S(2)}, u32[]{:S(2)}) collective-permute-start(bf16[32,1536]{1,0:T(8,128)(2,1)S(1)} %get-tuple-element.914), channel_id=1, source_target_pairs={{8,0},{16,8},{24,16},{9,1},{17,9},{25,17},{10,2},{18,10},{26,18},{... | collective-permute-start | bytes 294920 | tf_op jit(solution)/shard_map/while/body/eval_jaxpr/ppermute | solution.py:17
  222.1 6.5 %collective-permute-start = (bf16[32,1536]{1,0:T(8,128)(2,1)S(1)}, bf16[32,1536]{1,0:T(8,128)(2,1)S(1)}, u32[]{:S(2)}, u32[]{:S(2)}) collective-permute-start(bf16[32,1536]{1,0:T(8,128)(2,1)S(1)} %get-tuple-element.914), channel_id=1, source_target_pairs={{8,0},{16,8},{24,16},{9,1},{17,9},{25,17},{10,2},{18,10},{26,18},{... | collective-permute-start | bytes 294920 | tf_op jit(solution)/shard_map/while/body/eval_jaxpr/ppermute | solution.py:17
  228.6 19.6 %collective-permute-start = (bf16[32,1536]{1,0:T(8,128)(2,1)S(1)}, bf16[32,1536]{1,0:T(8,128)(2,1)S(1)}, u32[]{:S(2)}, u32[]{:S(2)}) collective-permute-start(bf16[32,1536]{1,0:T(8,128)(2,1)S(1)} %get-tuple-element.914), channel_id=1, source_target_pairs={{8,0},{16,8},{24,16},{9,1},{17,9},{25,17},{10,2},{18,10},{26,18},{... | collective-permute-start | bytes 294920 | tf_op jit(solution)/shard_map/while/body/eval_jaxpr/ppermute | solution.py:17
  253.3 6.5 %collective-permute-start = (bf16[32,1536]{1,0:T(8,128)(2,1)S(1)}, bf16[32,1536]{1,0:T(8,128)(2,1)S(1)}, u32[]{:S(2)}, u32[]{:S(2)}) collective-permute-start(bf16[32,1536]{1,0:T(8,128)(2,1)S(1)} %get-tuple-element.914), channel_id=1, source_target_pairs={{8,0},{16,8},{24,16},{9,1},{17,9},{25,17},{10,2},{18,10},{26,18},{... | collective-permute-start | bytes 294920 | tf_op jit(solution)/shard_map/while/body/eval_jaxpr/ppermute | solution.py:17
  264.9 6.5 %collective-permute-start = (bf16[32,1536]{1,0:T(8,128)(2,1)S(1)}, bf16[32,1536]{1,0:T(8,128)(2,1)S(1)}, u32[]{:S(2)}, u32[]{:S(2)}) collective-permute-start(bf16[32,1536]{1,0:T(8,128)(2,1)S(1)} %get-tuple-element.914), channel_id=1, source_target_pairs={{8,0},{16,8},{24,16},{9,1},{17,9},{25,17},{10,2},{18,10},{26,18},{... | collective-permute-start | bytes 294920 | tf_op jit(solution)/shard_map/while/body/eval_jaxpr/ppermute | solution.py:17
  276.5 6.5 %collective-permute-start = (bf16[32,1536]{1,0:T(8,128)(2,1)S(1)}, bf16[32,1536]{1,0:T(8,128)(2,1)S(1)}, u32[]{:S(2)}, u32[]{:S(2)}) collective-permute-start(bf16[32,1536]{1,0:T(8,128)(2,1)S(1)} %get-tuple-element.914), channel_id=1, source_target_pairs={{8,0},{16,8},{24,16},{9,1},{17,9},{25,17},{10,2},{18,10},{26,18},{... | collective-permute-start | bytes 294920 | tf_op jit(solution)/shard_map/while/body/eval_jaxpr/ppermute | solution.py:17
  288.1 6.5 %collective-permute-start = (bf16[32,1536]{1,0:T(8,128)(2,1)S(1)}, bf16[32,1536]{1,0:T(8,128)(2,1)S(1)}, u32[]{:S(2)}, u32[]{:S(2)}) collective-permute-start(bf16[32,1536]{1,0:T(8,128)(2,1)S(1)} %get-tuple-element.914), channel_id=1, source_target_pairs={{8,0},{16,8},{24,16},{9,1},{17,9},{25,17},{10,2},{18,10},{26,18},{... | collective-permute-start | bytes 294920 | tf_op jit(solution)/shard_map/while/body/eval_jaxpr/ppermute | solution.py:17
  299.7 6.5 %collective-permute-start = (bf16[32,1536]{1,0:T(8,128)(2,1)S(1)}, bf16[32,1536]{1,0:T(8,128)(2,1)S(1)}, u32[]{:S(2)}, u32[]{:S(2)}) collective-permute-start(bf16[32,1536]{1,0:T(8,128)(2,1)S(1)} %get-tuple-element.914), channel_id=1, source_target_pairs={{8,0},{16,8},{24,16},{9,1},{17,9},{25,17},{10,2},{18,10},{26,18},{... | collective-permute-start | bytes 294920 | tf_op jit(solution)/shard_map/while/body/eval_jaxpr/ppermute | solution.py:17
  311.4 6.8 %collective-permute-start = (bf16[32,1536]{1,0:T(8,128)(2,1)S(1)}, bf16[32,1536]{1,0:T(8,128)(2,1)S(1)}, u32[]{:S(2)}, u32[]{:S(2)}) collective-permute-start(bf16[32,1536]{1,0:T(8,128)(2,1)S(1)} %get-tuple-element.914), channel_id=1, source_target_pairs={{8,0},{16,8},{24,16},{9,1},{17,9},{25,17},{10,2},{18,10},{26,18},{... | collective-permute-start | bytes 294920 | tf_op jit(solution)/shard_map/while/body/eval_jaxpr/ppermute | solution.py:17
  323.3 7.1 %collective-permute-start = (bf16[32,1536]{1,0:T(8,128)(2,1)S(1)}, bf16[32,1536]{1,0:T(8,128)(2,1)S(1)}, u32[]{:S(2)}, u32[]{:S(2)}) collective-permute-start(bf16[32,1536]{1,0:T(8,128)(2,1)S(1)} %get-tuple-element.914), channel_id=1, source_target_pairs={{8,0},{16,8},{24,16},{9,1},{17,9},{25,17},{10,2},{18,10},{26,18},{... | collective-permute-start | bytes 294920 | tf_op jit(solution)/shard_map/while/body/eval_jaxpr/ppermute | solution.py:17
  335.5 6.5 %collective-permute-start = (bf16[32,1536]{1,0:T(8,128)(2,1)S(1)}, bf16[32,1536]{1,0:T(8,128)(2,1)S(1)}, u32[]{:S(2)}, u32[]{:S(2)}) collective-permute-start(bf16[32,1536]{1,0:T(8,128)(2,1)S(1)} %get-tuple-element.914), channel_id=1, source_target_pairs={{8,0},{16,8},{24,16},{9,1},{17,9},{25,17},{10,2},{18,10},{26,18},{... | collective-permute-start | bytes 294920 | tf_op jit(solution)/shard_map/while/body/eval_jaxpr/ppermute | solution.py:17
Sparse Core Ops, SparseCore 0:
  137.0 73.7 all-reduce.1
  343.2 20.8 reduce-scatter.1
where the time goes:
time: 375 us; the launch traced here: 372 us
  waiting for transfers between devices  179 us (48%)
  starting transfers between devices  63.5 us (17%)
  matrix products  52.1 us (14%)
  other arithmetic  32.3 us (9%)
  blocking collectives  21.3 us (6%)
  between operations  17.2 us (5%)
  local copies, waits for them, and re-layouts  4.94 us (1%)
    ppermute x22, waiting for transfers between devices, from_behind(): lax.ppermute(value, axis, [(source, source + steps) for source in range(f...  95 us
    psum x1, waiting for transfers between devices, shards(): lax.psum(block_gram(all_pre_act, batch_mean, BLOCK), 'batch') / row_total  73.7 us
    ppermute x22, starting transfers between devices, from_behind(): lax.ppermute(value, axis, [(source, source + steps) for source in range(f...  63.4 us
    dot_general x8, matrix products, backward_active_step(): jnp.einsum('rbi,bij->rbj', centered, deviation, precision=HIGHEST)  30.5 us
    dot_general x17, matrix products, group_forward(): jnp.einsum('rgi,gio->rgo', pieces, weight, preferred_element_type=jnp.flo...  14.5 us
    psum x1, blocking collectives, shards(): total_sum = lax.psum(sum_pre, 'batch')  12.2 us
    another operation x32, other arithmetic  11.8 us
    dynamic_update_slice x11, other arithmetic, forward_tick(): lax.dynamic_update_index_in_dim(stored, jnp.where(in_range, hidden, previ...  10.3 us
  transfers between devices with their start and end apart: 24, of which 24 were waited for; matrix products, arithmetic and copies ran while one was open for 0% of the time, Pallas kernels for 0%

commit v1 on v0

v1 whole, which is shorter than its diff:
```python
import functools

import jax
import jax.numpy as jnp
from jax import lax
from jax.experimental import pallas as pl
from jax.experimental.pallas import tpu as pltpu
from jax.sharding import PartitionSpec as P

BLOCK = 512
GROUP = 256
HALF = 128
WIDE = GROUP + HALF
LAG = (0, 0, 0, 1, 2, 3, 4, 4)
EPS = 1e-05
MESH = pl.DeviceIdType.MESH
F32 = jnp.float32
BF16 = jnp.bfloat16


def dot(a, b, dims):
    return lax.dot_general(a, b, (dims, ((), ())), preferred_element_type=F32)


def kernel(nl, nb, nj, x_ref, w_ref, mean_ref, var_ref, gain_ref, bias_ref, out_ref, loss_ref,
           wall, ss, xbuf, zall, slope, zc, sacc, srs, rs, e, psend, pall, mub, mu_all, lossb, lossz,
           z_s, z_r, ss_s, ss_r, w2_s, w2_r, w3_s, w3_r, zc_s, zc_r, mu_s, mu_r, rs_s, rs_r,
           ag_s, ag_r, ex_s, ex_r, pu_s, pu_r, lb_s, lb_r, lz_s, lz_r):
    s = lax.axis_index("section")
    b = lax.axis_index("batch")
    chip, core = b // 2, b % 2
    nc = nb // 2
    mate = chip * 2 + (1 - core)
    rows = x_ref.shape[0]
    own_rows = rows // nl
    piece = GROUP // nc
    row_total = rows * nb

    def copy(src, dst, ssem, rsem, sec, bat):
        return pltpu.make_async_remote_copy(
            src_ref=src, dst_ref=dst, send_sem=ssem, recv_sem=rsem,
            device_id=(sec, bat), device_id_type=MESH)

    def each(count, me, body):
        def step(k, carry):
            body(k, lax.rem(me + k, count))
            return carry
        lax.fori_loop(1, count, step, 0)

    def z_copy(j, k, q):
        return copy(w_ref.at[j, chip, core], wall.at[s, j, chip, core], z_s.at[j, k], z_r.at[j, s], q, b)

    def z_wait(j, l):
        d = wall.at[l, j, chip, core]
        copy(d, d, z_s.at[j, 0], z_r.at[j, l], l, b).wait_recv()

    def ss_copy(k, q):
        return copy(ss.at[s], ss.at[s], ss_s.at[k], ss_r.at[s], q, b)

    def w2_copy(l, j, k, q):
        d = wall.at[l, j, chip, core]
        return copy(d, d, w2_s.at[l, j, k], w2_r.at[l, j, chip], s, q * 2 + core)

    def w3_copy(l, j, half):
        d = wall.at[l, j, :, half]
        return copy(d, d, w3_s.at[l, j], w3_r.at[l, j], s, mate)

    def zc_copy(j, half):
        return copy(zc.at[j, half], zc.at[j, half], zc_s.at[j], zc_r.at[j], s, mate)

    def mu_copy(j, k, q):
        return copy(mub.at[j, b], mub.at[j, b], mu_s.at[j, k], mu_r.at[j, b], s, q)

    def rs_copy(j, k, q):
        return copy(srs.at[j, q], rs.at[j, chip], rs_s.at[j, k], rs_r.at[j, chip], s, q * 2 + core)

    def ag_copy(j, k, q):
        d = e.at[j, core, chip]
        return copy(d, d, ag_s.at[j, k], ag_r.at[j, chip], s, q * 2 + core)

    def ex_copy(j, half):
        return copy(e.at[j, half], e.at[j, half], ex_s.at[j], ex_r.at[j], s, mate)

    def pu_copy(j, k, q):
        return copy(psend.at[j, q], pall.at[s, j], pu_s.at[j, k], pu_r.at[j, s], q, b)

    def lb_copy(k, q):
        return copy(lossb.at[b], lossb.at[b], lb_s.at[k], lb_r.at[b], s, q)

    def lz_copy(k, q):
        return copy(lossz.at[s], lossz.at[s], lz_s.at[k], lz_r.at[s], q, b)

    barrier = pltpu.get_barrier_semaphore()
    each(nb, b, lambda k, q: pl.semaphore_signal(barrier, inc=1, device_id=(s, q), device_id_type=MESH))
    each(nl, s, lambda k, q: pl.semaphore_signal(barrier, inc=1, device_id=(q, b), device_id_type=MESH))
    scale_own = gain_ref[...] * lax.rsqrt(var_ref[...] + EPS)
    ss[s, 0:1, :] = 0.5 * scale_own
    ss[s, 1:2, :] = 0.5 * (bias_ref[...] - mean_ref[...] * scale_own)
    for j in range(nj):
        wall[s, j] = w_ref[j]
    pl.semaphore_wait(barrier, nb - 1 + nl - 1)

    each(nl, s, lambda k, q: ss_copy(k, q).start())
    for j in range(nj):
        each(nl, s, lambda k, q: z_copy(j, k, q).start())

    def spread_chips(j):
        def one(_, l):
            z_wait(j, l)
            each(nc, chip, lambda k, q: w2_copy(l, j, k, q).start())
        each(nl, s, one)

    def spread_mate(j):
        def one(_, l):
            def arrived(k, q):
                d = wall.at[l, j, q, core]
                copy(d, d, w2_s.at[l, j, 0], w2_r.at[l, j, q], s, q * 2 + core).wait_recv()
            each(nc, chip, arrived)
            w3_copy(l, j, core).start()
        each(nl, s, one)

    def forward(j):
        cols = slice(j * BLOCK, (j + 1) * BLOCK)
        xbuf[...] = x_ref[:, cols]

        def layer(l, carry):
            @pl.when(l != s)
            def _():
                w3_copy(l, j, 1 - core).wait_recv()
                if j == 0:
                    copy(ss.at[l], ss.at[l], ss_s.at[0], ss_r.at[l], l, b).wait_recv()
            w = wall[l, j].reshape(BLOCK, GROUP)
            for g in range(BLOCK // GROUP):
                part = slice(g * GROUP, (g + 1) * GROUP)
                lanes = slice(j * BLOCK + g * GROUP, j * BLOCK + (g + 1) * GROUP)
                z = dot(xbuf[:, part], w[part], ((1,), (0,)))
                zall[l, j, :, part] = z
                half = z * ss[l, 0:1, lanes] + ss[l, 1:2, lanes]
                xbuf[:, part] = (half + half * jnp.tanh(half)).astype(BF16)
            return carry
        lax.fori_loop(0, nl, layer, 0)
        z = zall[s, j]
        mu = jnp.sum(z, axis=0, keepdims=True) * (1.0 / rows)
        mub[j, b] = mu
        each(nb, b, lambda k, q: mu_copy(j, k, q).start())
        centered = (z - mu).astype(BF16)
        for h in range(BLOCK // GROUP):
            zc[j, core, h] = centered[:, h * GROUP:(h + 1) * GROUP]
        zc_copy(j, core).start()

    def gram(j):
        zc_copy(j, 1 - core).wait_recv()
        cross = pl.ds(pl.multiple_of(core * HALF, HALF), HALF)
        square = dot(zc[j, 0, core], zc[j, 0, core], ((0,), (0,))) + dot(
            zc[j, 1, core], zc[j, 1, core], ((0,), (0,)))
        other = dot(zc[j, 0, 0], zc[j, 0, 1, :, cross], ((0,), (0,))) + dot(
            zc[j, 1, 0], zc[j, 1, 1, :, cross], ((0,), (0,)))
        total = jnp.concatenate([square, other], axis=1).reshape(nc, piece, WIDE)
        sacc[j] = total
        srs[j] = total.astype(BF16)
        each(nc, chip, lambda k, q: rs_copy(j, k, q).start())

    def batch_mean(j):
        return jnp.sum(mub[j], axis=0) * (1.0 / nb)

    def reduce(j):
        cols = slice(j * BLOCK, (j + 1) * BLOCK)

        def arrived_mu(k, q):
            copy(mub.at[j, q], mub.at[j, q], mu_s.at[j, 0], mu_r.at[j, q], s, q).wait_recv()
        each(nb, b, arrived_mu)
        mu = batch_mean(j)
        mine = pl.ds(pl.multiple_of(core * GROUP, GROUP), GROUP)
        cross = pl.ds(pl.multiple_of(GROUP + core * HALF, HALF), HALF)
        var_lanes = pl.ds(pl.multiple_of(j * BLOCK + core * GROUP, GROUP), GROUP)
        mu_all[...] = mu
        mu_mine, mu_cross, mu_low = mu_all[:, mine], mu_all[:, cross], mu[:, :GROUP]
        eye = (lax.broadcasted_iota(jnp.int32, (piece, GROUP), 0) + chip * piece
               == lax.broadcasted_iota(jnp.int32, (piece, GROUP), 1)).astype(F32)

        def between(i, acc):
            low = mub[j, i, :, :GROUP] - mu_low
            d_mine = mub[j, i, :, mine] - mu_mine
            d_cross = mub[j, i, :, cross] - mu_cross
            column = jnp.sum(eye * d_mine, axis=1, keepdims=True)
            column_low = jnp.sum(eye * low, axis=1, keepdims=True)
            return (acc[0] + column * d_mine, acc[1] + column_low * d_cross)
        corr = jnp.concatenate(lax.fori_loop(
            0, nb, between, (jnp.zeros((piece, GROUP), F32), jnp.zeros((piece, HALF), F32))), axis=1)
        sacc[j, chip] = sacc[j, chip] + corr * rows

        def arrived(k, q):
            copy(rs.at[j, q], rs.at[j, q], rs_s.at[j, 0], rs_r.at[j, q], s, q * 2 + core).wait_recv()
            sacc[j, chip] = sacc[j, chip] + rs[j, q].astype(F32)
        each(nc, chip, arrived)
        cov = sacc[j, chip] * (1.0 / row_total)
        dev, dev_cross = cov[:, :GROUP] - eye * var_ref[:, var_lanes], cov[:, GROUP:]
        e[j, core, chip] = jnp.concatenate([dev, dev_cross], axis=1).astype(BF16)
        each(nc, chip, lambda k, q: ag_copy(j, k, q).start())
        square = jnp.sum((dev * dev).reshape(piece // 8, 8, GROUP), axis=0) * 0.25
        double = jnp.sum((dev_cross * dev_cross).reshape(piece // 8, 8, HALF), axis=0) * 0.5
        off = mu - mean_ref[:, cols]
        off = off * off
        off = sum(off[:, i * HALF:(i + 1) * HALF] for i in range(BLOCK // HALF))
        head = (lax.broadcasted_iota(jnp.int32, (8, HALF), 0) + b == 0).astype(F32)
        tile = square[:, :HALF] + square[:, HALF:] + double + head * off
        if j == 0:
            lossb[b] = tile
        else:
            lossb[b] = lossb[b] + tile
        if j == nj - 1:
            each(nb, b, lambda k, q: lb_copy(k, q).start())

    def swap(j):
        def arrived(k, q):
            d = e.at[j, core, q]
            copy(d, d, ag_s.at[j, 0], ag_r.at[j, q], s, q * 2 + core).wait_recv()
        each(nc, chip, arrived)
        ex_copy(j, core).start()

    def pull(j):
        cols = slice(j * BLOCK, (j + 1) * BLOCK)
        mu = batch_mean(j)
        ex_copy(j, 1 - core).wait_recv()
        c0 = (zall[s, j, :, :GROUP] - mu[:, :GROUP]).astype(BF16)
        c1 = (zall[s, j, :, GROUP:] - mu[:, GROUP:]).astype(BF16)
        e0, e1 = e[j, 0].reshape(GROUP, WIDE), e[j, 1].reshape(GROUP, WIDE)
        cross = jnp.concatenate([e0[:, GROUP:], e1[:, GROUP:]], axis=1)
        p0 = dot(c0, e0[:, :GROUP], ((1,), (0,))) + dot(c1, cross, ((1,), (1,)))
        p1 = dot(c0, cross, ((1,), (0,))) + dot(c1, e1[:, :GROUP], ((1,), (0,)))
        p = jnp.concatenate([p0, p1], axis=1) + 2.0 * (mu - mean_ref[:, cols])
        psend[j] = p.astype(BF16).reshape(nl, own_rows, BLOCK)
        each(nl, s, lambda k, q: pu_copy(j, k, q).start())
        pall[s, j] = psend[j, s]

    def slopes(j):
        cols = slice(j * BLOCK, (j + 1) * BLOCK)

        def layer(l, carry):
            scale = ss[l, 0:1, cols]
            half = zall[l, j, pl.ds(pl.multiple_of(s * own_rows, own_rows), own_rows), :] * scale + ss[l, 1:2, cols]
            t = jnp.tanh(half)
            slope[l, j] = (1.0 + t) * (1.0 + half * (1.0 - t)) * scale
            return carry
        lax.fori_loop(0, nl, layer, 0)

    def backward(j):
        cols = slice(j * BLOCK, (j + 1) * BLOCK)

        def layer(i, up):
            l = nl - 1 - i

            @pl.when(l != s)
            def _():
                d = pall.at[l, j]
                copy(d, d, pu_s.at[j, 0], pu_r.at[j, l], l, b).wait_recv()
            grad = (up * slope[l, j] + pall[l, j].astype(F32)).astype(BF16)
            w = wall[l, j].reshape(BLOCK, GROUP)
            parts = []
            for g in range(BLOCK // GROUP):
                part = slice(g * GROUP, (g + 1) * GROUP)
                parts.append(dot(grad[:, part], w[part], ((1,), (1,))))
            return jnp.concatenate(parts, axis=1).astype(BF16).astype(F32)
        up = lax.fori_loop(0, nl, layer, jnp.zeros((own_rows, BLOCK), F32))
        out_ref[:, cols] = up.astype(BF16)

    def loss_plane():
        def arrived(k, q):
            copy(lossb.at[q], lossb.at[q], lb_s.at[0], lb_r.at[q], s, q).wait_recv()
        each(nb, b, arrived)
        lossz[s] = jnp.sum(lossb[...], axis=0)
        each(nl, s, lambda k, q: lz_copy(k, q).start())

    def loss_all():
        def arrived(k, q):
            copy(lossz.at[q], lossz.at[q], lz_s.at[0], lz_r.at[q], q, b).wait_recv()
        each(nl, s, arrived)
        total = jnp.sum(jnp.sum(lossz[...], axis=0), axis=(0, 1), keepdims=True)
        loss_ref[...] = jnp.broadcast_to(total * (1.0 / (nl * nj * BLOCK)), loss_ref.shape)

    def early_sends():
        each(nl, s, lambda k, q: ss_copy(k, q).wait_send())

        def block_sends(j, carry):
            each(nl, s, lambda k, q: z_copy(j, k, q).wait_send())
            each(nb, b, lambda k, q: mu_copy(j, k, q).wait_send())
            each(nc, chip, lambda k, q: rs_copy(j, k, q).wait_send())
            each(nc, chip, lambda k, q: ag_copy(j, k, q).wait_send())
            zc_copy(j, core).wait_send()
            ex_copy(j, core).wait_send()

            def weight_sends(_, l):
                each(nc, chip, lambda k, q: w2_copy(l, j, k, q).wait_send())
                w3_copy(l, j, core).wait_send()
            each(nl, s, weight_sends)
            return carry
        lax.fori_loop(0, nj, block_sends, 0)

    lead = (spread_chips, spread_mate, forward, gram, reduce, swap, pull, slopes)
    order = []
    for t in range(nj + 5):
        for stage, delay in zip(lead, LAG):
            if 0 <= t - delay < nj:
                order.append((stage, t - delay))
    Z, M, F, C, E, X, Q, S, B = lead + (backward,)
    if nj == 3:
        order = [(Z, 0), (Z, 1), (M, 0), (F, 0), (Z, 2), (M, 1), (C, 0), (F, 1), (M, 2), (C, 1), (F, 2), (E, 0),
                 (C, 2), (X, 0), (E, 1), (Q, 0), (X, 1), (E, 2), (Q, 1), (S, 0), (S, 1), (S, 2), (B, 0),
                 (X, 2), (Q, 2)]
    else:
        order += [(B, 0)]
    for stage, j in order:
        stage(j)
    loss_plane()
    early_sends()
    for j in range(1, nj):
        backward(j)
    loss_all()
    each(nl, s, lambda k, q: lz_copy(k, q).wait_send())
    each(nb, b, lambda k, q: lb_copy(k, q).wait_send())
    for j in range(nj):
        each(nl, s, lambda k, q: pu_copy(j, k, q).wait_send())


def shards(nl, nb, images, weights, bn_mean, bn_var, bn_gain, bn_bias):
    rows, channels = images.shape[1:]
    nj = channels // BLOCK
    nc = nb // 2
    own_rows = rows // nl
    piece = GROUP // nc
    vmem, dma = pltpu.VMEM, pltpu.SemaphoreType.DMA
    halves = BLOCK // GROUP
    sems = []
    for shape in ((nj, nl), (nl,), (nl, nj, nc), (nl, nj), (nj,), (nj, nb), (nj, nc), (nj, nc),
                  (nj,), (nj, nl), (nb,), (nl,)):
        sems += [dma(shape), dma(shape)]
    out, loss = pl.pallas_call(
        functools.partial(kernel, nl, nb, nj),
        out_shape=(jax.ShapeDtypeStruct((own_rows, channels), BF16),
                   jax.ShapeDtypeStruct((8, 128), F32)),
        in_specs=[pl.BlockSpec(memory_space=vmem)] * 6,
        out_specs=(pl.BlockSpec(memory_space=vmem),) * 2,
        scratch_shapes=[
            vmem((nl, nj, nc, 2, BLOCK // nb, GROUP), BF16),
            vmem((nl, 2, channels), F32),
            vmem((rows, BLOCK), BF16),
            vmem((nl, nj, rows, BLOCK), F32),
            vmem((nl, nj, own_rows, BLOCK), F32),
            vmem((nj, 2, halves, rows, GROUP), BF16),
            vmem((nj, nc, piece, WIDE), F32),
            vmem((nj, nc, piece, WIDE), BF16),
            vmem((nj, nc, piece, WIDE), BF16),
            vmem((nj, 2, nc, piece, WIDE), BF16),
            vmem((nj, nl, own_rows, BLOCK), BF16),
            vmem((nl, nj, own_rows, BLOCK), BF16),
            vmem((nj, nb, 1, BLOCK), F32),
            vmem((1, BLOCK), F32),
            vmem((nb, 8, 128), F32),
            vmem((nl, 8, 128), F32),
        ] + sems,
        compiler_params=pltpu.CompilerParams(
            collective_id=0, has_side_effects=True, vmem_limit_bytes=60 * 1024 * 1024),
    )(images[0], weights.reshape(nj, nc, 2, BLOCK // nb, GROUP), bn_mean, bn_var, bn_gain, bn_bias)
    return (out[None], loss[0, 0])


def solution(mesh):
    placed = (
        P("batch", None, None),
        P("section", None, None, None),
        P("section", None),
        P("section", None),
        P("section", None),
        P("section", None),
    )
    return jax.shard_map(
        functools.partial(shards, mesh.shape["section"], mesh.shape["batch"]),
        mesh=mesh,
        in_specs=placed,
        out_specs=(P("batch", "section", None), P()),
        check_vma=False,
    )
```

time: 375 us -> 65.4 us (0.17)
  waiting for transfers between devices: 179 us -> 0 us
  starting transfers between devices: 63.5 us -> 0 us
  Pallas kernels: 0 us -> 61.7 us
  matrix products: 52.1 us -> 0 us
  other arithmetic: 32.3 us -> 0 us
  blocking collectives: 21.3 us -> 0 us
  between operations: 17.2 us -> 0.64 us
    ppermute x22 -> x0, waiting for transfers between devices: 95 us -> none  [from_behind(): lax.ppermute(value, axis, [(source, source + steps) for source in range(f...]
    psum x1 -> x0, waiting for transfers between devices: 73.7 us -> none  [shards(): lax.psum(block_gram(all_pre_act, batch_mean, BLOCK), 'batch') / row_total]
    ppermute x22 -> x0, starting transfers between devices: 63.4 us -> none  [from_behind(): lax.ppermute(value, axis, [(source, source + steps) for source in range(f...]
    pallas_call x0 -> x1, Pallas kernels: none -> 61.7 us  [shards(): pl.pallas_call(functools.partial(kernel, nl, nb, nj), out_shape=(jax.Shap...]
    dot_general x34 -> x0, matrix products: 52.1 us -> none  [the longest x8 30.5 us: backward_active_step(): jnp.einsum('rbi,bij->rbj', centered, deviation, precision=HIGHEST)]
    psum x2 -> x0, blocking collectives: 21.3 us -> none  [the longest x1 12.2 us: shards(): total_sum = lax.psum(sum_pre, 'batch')]
    another operation x32 -> x0, other arithmetic: 11.8 us -> none
    dynamic_update_slice x22 -> x0, other arithmetic: 10.6 us -> none  [the longest x11 10.3 us: forward_tick(): lax.dynamic_update_index_in_dim(stored, jnp.where(in_range, hidden, previ...]
  transfers between devices with their start and end apart: 24 -> 0, of which waited for: 24 -> 0; matrix products, arithmetic and copies ran while one was open for 0% -> 0% of each run, Pallas kernels for 0% -> 0%
where the time goes in v1:
time: 65.4 us; the launch traced here: 65.2 us
  Pallas kernels  61.7 us (94%)
  local copies, waits for them, and re-layouts  2.8 us (4%)
    pallas_call x1, Pallas kernels, shards(): pl.pallas_call(functools.partial(kernel, nl, nb, nj), out_shape=(jax.Shap...  61.7 us
    unnamed x1, local copies, waits for them, and re-layouts  1.62 us

profile of v1, /device:TPU:0, one launch (start us, length us, event | category | flops | bytes accessed | tf_op | source)
XLA Modules:
  0.0 65.2 jit_solution(2286578159672552338)
XLA Ops:
  0.6 61.7 %shard_map.77 = (bf16[64,1536]{1,0:T(8,128)(2,1)}, f32[8,128]{1,0:T(8,128)}) custom-call(bf16[256,1536]{1,0:T(8,128)(2,1)} %bitcast.4, bf16[3,4,2,64,256]{4,3,2,1,0:T(8,128)(2,1)} %bitcast.5, f32[1,1536]{1,0:T(1,128)} %mean_ref.1, f32[1,1536]{1,0:T(1,128)} %var_ref.1, f32[1,1536]{1,0:T(1,128)} %gain_ref.1, f32[1,1536]{1,0:T(1,128)} %bias_ref.1), custom_call_target="tpu_custom_call" | custom-call | tf_op jit(solution)/shard_map/pallas_call | solution.py:337
  62.4 1.2 %slice.3 = f32[1,1]{1,0:T(1,128)} slice(f32[8,128]{1,0:T(8,128)} %get-tuple-element.5), slice={[0:1], [0:1]} | slice | bytes 8 | tf_op jit(solution)/shard_map/slice | solution.py:364
  63.6 1.6 %copy.9 = bf16[1,64,1536]{2,1,0:T(8,128)(2,1)} copy(bf16[1,64,1536]{2,1,0:T(8,128)(2,1)} %bitcast.6) | data formatting | bytes 393216

commit v2 on v1

--- a/solution.py
+++ b/solution.py
@@ -11,7 +11,6 @@
 GROUP = 256
 HALF = 128
 WIDE = GROUP + HALF
-LAG = (0, 0, 0, 1, 2, 3, 4, 4)
 EPS = 1e-05
 MESH = pl.DeviceIdType.MESH
 F32 = jnp.float32
@@ -275,8 +274,7 @@
         def arrived(k, q):
             copy(lossz.at[q], lossz.at[q], lz_s.at[0], lz_r.at[q], q, b).wait_recv()
         each(nl, s, arrived)
-        total = jnp.sum(jnp.sum(lossz[...], axis=0), axis=(0, 1), keepdims=True)
-        loss_ref[...] = jnp.broadcast_to(total * (1.0 / (nl * nj * BLOCK)), loss_ref.shape)
+        loss_ref[0, 0] = jnp.sum(jnp.sum(lossz[...], axis=0)) * (1.0 / (nl * nj * BLOCK))
 
     def early_sends():
         each(nl, s, lambda k, q: ss_copy(k, q).wait_send())
@@ -296,19 +294,10 @@
             return carry
         lax.fori_loop(0, nj, block_sends, 0)
 
-    lead = (spread_chips, spread_mate, forward, gram, reduce, swap, pull, slopes)
-    order = []
-    for t in range(nj + 5):
-        for stage, delay in zip(lead, LAG):
-            if 0 <= t - delay < nj:
-                order.append((stage, t - delay))
-    Z, M, F, C, E, X, Q, S, B = lead + (backward,)
-    if nj == 3:
-        order = [(Z, 0), (Z, 1), (M, 0), (F, 0), (Z, 2), (M, 1), (C, 0), (F, 1), (M, 2), (C, 1), (F, 2), (E, 0),
-                 (C, 2), (X, 0), (E, 1), (Q, 0), (X, 1), (E, 2), (Q, 1), (S, 0), (S, 1), (S, 2), (B, 0),
-                 (X, 2), (Q, 2)]
-    else:
-        order += [(B, 0)]
+    Z, M, F, C, E, X, Q, S, B = (
+        spread_chips, spread_mate, forward, gram, reduce, swap, pull, slopes, backward)
+    order = [(Z, 0), (M, 0), (F, 0), (Z, 1), (C, 0), (M, 1), (F, 1), (E, 0), (Z, 2), (C, 1), (X, 0), (Q, 0),
+             (M, 2), (F, 2), (E, 1), (C, 2), (X, 1), (Q, 1), (E, 2), (S, 0), (S, 1), (S, 2), (B, 0), (X, 2), (Q, 2)]
     for stage, j in order:
         stage(j)
     loss_plane()
@@ -337,9 +326,9 @@
     out, loss = pl.pallas_call(
         functools.partial(kernel, nl, nb, nj),
         out_shape=(jax.ShapeDtypeStruct((own_rows, channels), BF16),
-                   jax.ShapeDtypeStruct((8, 128), F32)),
+                   jax.ShapeDtypeStruct((1, 1), F32)),
         in_specs=[pl.BlockSpec(memory_space=vmem)] * 6,
-        out_specs=(pl.BlockSpec(memory_space=vmem),) * 2,
+        out_specs=(pl.BlockSpec(memory_space=vmem), pl.BlockSpec(memory_space=pltpu.SMEM)),
         scratch_shapes=[
             vmem((nl, nj, nc, 2, BLOCK // nb, GROUP), BF16),
             vmem((nl, 2, channels), F32),
@@ -361,7 +350,7 @@
         compiler_params=pltpu.CompilerParams(
             collective_id=0, has_side_effects=True, vmem_limit_bytes=60 * 1024 * 1024),
     )(images[0], weights.reshape(nj, nc, 2, BLOCK // nb, GROUP), bn_mean, bn_var, bn_gain, bn_bias)
-    return (out[None], loss[0, 0])
+    return (out[None], loss.reshape(()))
 
 
 def solution(mesh):

time: 65.4 us -> 70.9 us (1.084)
  Pallas kernels: 61.7 us -> 66.7 us
  between operations: 0.64 us -> 2.4 us
  local copies, waits for them, and re-layouts: 2.8 us -> 1.62 us
    pallas_call x1, Pallas kernels: 61.7 us -> 66.7 us  [shards(): pl.pallas_call(functools.partial(kernel, nl, nb, nj), out_shape=(jax.Shap...]
    slice x1 -> x0, local copies, waits for them, and re-layouts: 1.18 us -> none  [shards(): return (out[None], loss[0, 0])]
where the time goes in v2:
time: 70.9 us; the launch traced here: 70.7 us
  Pallas kernels  66.7 us (94%)
  between operations  2.4 us (3%)
  local copies, waits for them, and re-layouts  1.62 us (2%)
    pallas_call x1, Pallas kernels, shards(): pl.pallas_call(functools.partial(kernel, nl, nb, nj), out_shape=(jax.Shap...  66.7 us
    unnamed x1, local copies, waits for them, and re-layouts  1.62 us

profile of v2, /device:TPU:0, one launch (start us, length us, event | category | flops | bytes accessed | tf_op | source)
XLA Modules:
  0.0 70.7 jit_solution(3681760384510653425)
XLA Ops:
  0.6 66.7 %shard_map.77 = (bf16[64,1536]{1,0:T(8,128)(2,1)}, f32[1,1]{1,0:T(1,128)}) custom-call(bf16[256,1536]{1,0:T(8,128)(2,1)} %bitcast.4, bf16[3,4,2,64,256]{4,3,2,1,0:T(8,128)(2,1)} %bitcast.5, f32[1,1536]{1,0:T(1,128)} %mean_ref.1, f32[1,1536]{1,0:T(1,128)} %var_ref.1, f32[1,1536]{1,0:T(1,128)} %gain_ref.1, f32[1,1536]{1,0:T(1,128)} %bias_ref.1), custom_call_target="tpu_custom_call" | custom-call | tf_op jit(solution)/shard_map/pallas_call | solution.py:326
  67.3 1.6 %copy.10 = bf16[1,64,1536]{2,1,0:T(8,128)(2,1)} copy(bf16[1,64,1536]{2,1,0:T(8,128)(2,1)} %bitcast.6) | data formatting | bytes 393216

commit v3 on v2

v3 whole, which is shorter than its diff:
```python
import functools

import jax
import jax.numpy as jnp
from jax import lax
from jax.experimental import pallas as pl
from jax.experimental.pallas import tpu as pltpu
from jax.sharding import PartitionSpec as P

BLOCK = 512
GROUP = 256
HALF = 128
WIDE = GROUP + HALF
EPS = 1e-05
MESH = pl.DeviceIdType.MESH
F32 = jnp.float32
BF16 = jnp.bfloat16


def dot(a, b, dims):
    return lax.dot_general(a, b, (dims, ((), ())), preferred_element_type=F32)


def kernel(nl, nb, nj, x_ref, w_ref, mean_ref, var_ref, gain_ref, bias_ref, out_ref, loss_ref,
           wall, ss, xbuf, zall, slope, zc, sacc, srs, rs, e, psend, pall, mub, mu_all, lossb, lossz,
           send, recv):
    s = lax.axis_index("section")
    b = lax.axis_index("batch")
    chip, core = b // 2, b % 2
    nc = nb // 2
    mate = chip * 2 + (1 - core)
    rows = x_ref.shape[0]
    own_rows = rows // nl
    piece = GROUP // nc
    row_total = rows * nb

    def copy(src, dst, ssem, rsem, sec, bat):
        return pltpu.make_async_remote_copy(
            src_ref=src, dst_ref=dst, send_sem=ssem, recv_sem=rsem,
            device_id=(sec, bat), device_id_type=MESH)

    def each(count, me, body):
        if count <= 8:
            for k in range(1, count):
                body(k, lax.rem(me + k, count))
        else:
            def step(k, carry):
                body(k, lax.rem(me + k, count))
                return carry
            lax.fori_loop(1, count, step, 0)

    def loop(count, body, carry):
        if count > 8:
            return lax.fori_loop(0, count, body, carry)
        for i in range(count):
            carry = body(i, carry)
        return carry

    def slot(l):
        return lax.rem(l - s + nl, nl)

    SS, WZ, WC, WM, ZC, MM, MC, RS, AG, EX, PU, LB, LZ = range(13)

    def got(kind, j, ref):
        copy(ref, ref, send.at[kind], recv.at[kind, j], s, mate).wait_recv()

    def sent(kind, ref):
        copy(ref, ref, send.at[kind], recv.at[kind, 0], s, mate).wait_send()

    def put(kind, j, src, dst, sec, bat):
        copy(src, dst, send.at[kind], recv.at[kind, j], sec, bat).start()

    barrier = pltpu.get_barrier_semaphore()
    each(nb, b, lambda k, q: pl.semaphore_signal(barrier, inc=1, device_id=(s, q), device_id_type=MESH))
    each(nl, s, lambda k, q: pl.semaphore_signal(barrier, inc=1, device_id=(q, b), device_id_type=MESH))
    scale_own = gain_ref[...] * lax.rsqrt(var_ref[...] + EPS)
    ss[0, 0:1, :] = 0.5 * scale_own
    ss[0, 1:2, :] = 0.5 * (bias_ref[...] - mean_ref[...] * scale_own)
    for j in range(nj):
        wall[0, j] = w_ref[j]
    pl.semaphore_wait(barrier, nb - 1 + nl - 1)

    each(nl, s, lambda k, q: put(SS, 0, ss.at[0], ss.at[nl - k], q, b))
    for j in range(nj):
        each(nl, s, lambda k, q: put(WZ, j, w_ref.at[j, chip, core], wall.at[nl - k, j, chip, core], q, b))

    def spread_chips(j):
        mine = wall.at[pl.ds(1, nl - 1), j, chip, core]
        got(WZ, j, mine)
        each(nc, chip, lambda k, q: put(WC, j, mine, mine, s, q * 2 + core))

    def spread_mate(j):
        got(WC, j, wall.at[pl.ds(1, nl - 1), j, pl.ds(1, nc - 1), core])
        mine = wall.at[pl.ds(1, nl - 1), j, :, core]
        put(WM, j, mine, mine, s, mate)

    def forward(j):
        cols = slice(j * BLOCK, (j + 1) * BLOCK)
        got(WM, j, wall.at[pl.ds(1, nl - 1), j, :, 1 - core])
        if j == 0:
            got(SS, 0, ss.at[pl.ds(1, nl - 1)])
        xbuf[...] = x_ref[:, cols]

        def layer(l, carry):
            at = slot(l)
            w = wall[at, j].reshape(BLOCK, GROUP)
            for g in range(BLOCK // GROUP):
                part = slice(g * GROUP, (g + 1) * GROUP)
                lanes = slice(j * BLOCK + g * GROUP, j * BLOCK + (g + 1) * GROUP)
                z = dot(xbuf[:, part], w[part], ((1,), (0,)))
                zall[l, j, :, part] = z
                half = z * ss[at, 0:1, lanes] + ss[at, 1:2, lanes]
                xbuf[:, part] = (half + half * jnp.tanh(half)).astype(BF16)
            return carry
        loop(nl, layer, 0)
        z = zall[s, j]
        mu = jnp.sum(z, axis=0, keepdims=True) * (1.0 / rows)
        mub[j, chip, core] = mu
        put(MM, j, mub.at[j, chip, core], mub.at[j, chip, core], s, mate)
        centered = (z - mu).astype(BF16)
        for h in range(BLOCK // GROUP):
            zc[j, core, h] = centered[:, h * GROUP:(h + 1) * GROUP]
        put(ZC, j, zc.at[j, core], zc.at[j, core], s, mate)

    def gram(j):
        got(MM, j, mub.at[j, chip, 1 - core])
        each(nc, chip, lambda k, q: put(MC, j, mub.at[j, chip], mub.at[j, chip], s, q * 2 + core))
        got(ZC, j, zc.at[j, 1 - core])
        cross = pl.ds(pl.multiple_of(core * HALF, HALF), HALF)
        square = dot(zc[j, 0, core], zc[j, 0, core], ((0,), (0,))) + dot(
            zc[j, 1, core], zc[j, 1, core], ((0,), (0,)))
        other = dot(zc[j, 0, 0], zc[j, 0, 1, :, cross], ((0,), (0,))) + dot(
            zc[j, 1, 0], zc[j, 1, 1, :, cross], ((0,), (0,)))
        total = jnp.concatenate([square, other], axis=1).reshape(nc, piece, WIDE)
        sacc[j] = total
        srs[j] = total.astype(BF16)
        each(nc, chip, lambda k, q: put(RS, j, srs.at[j, q], rs.at[j, nc - k], s, q * 2 + core))

    def batch_mean(j):
        return jnp.sum(mub[j], axis=(0, 1)) * (1.0 / nb)

    def reduce(j):
        cols = slice(j * BLOCK, (j + 1) * BLOCK)

        got(MC, j, mub.at[j, pl.ds(1, nc - 1)])
        mu = batch_mean(j)
        mine = pl.ds(pl.multiple_of(core * GROUP, GROUP), GROUP)
        cross = pl.ds(pl.multiple_of(GROUP + core * HALF, HALF), HALF)
        var_lanes = pl.ds(pl.multiple_of(j * BLOCK + core * GROUP, GROUP), GROUP)
        mu_all[...] = mu
        mu_mine, mu_cross, mu_low = mu_all[:, mine], mu_all[:, cross], mu[:, :GROUP]
        eye = (lax.broadcasted_iota(jnp.int32, (piece, GROUP), 0) + chip * piece
               == lax.broadcasted_iota(jnp.int32, (piece, GROUP), 1)).astype(F32)

        def between(i, acc):
            low = mub[j, i // 2, i % 2, :, :GROUP] - mu_low
            d_mine = mub[j, i // 2, i % 2, :, mine] - mu_mine
            d_cross = mub[j, i // 2, i % 2, :, cross] - mu_cross
            column = jnp.sum(eye * d_mine, axis=1, keepdims=True)
            column_low = jnp.sum(eye * low, axis=1, keepdims=True)
            return (acc[0] + column * d_mine, acc[1] + column_low * d_cross)
        corr = jnp.concatenate(loop(
            nb, between, (jnp.zeros((piece, GROUP), F32), jnp.zeros((piece, HALF), F32))), axis=1)
        cov = sacc[j, chip] + corr * rows
        got(RS, j, rs.at[j, pl.ds(1, nc - 1)])
        cov = loop(nc - 1, lambda i, acc: acc + rs[j, i + 1].astype(F32), cov) * (1.0 / row_total)
        dev, dev_cross = cov[:, :GROUP] - eye * var_ref[:, var_lanes], cov[:, GROUP:]
        e[j, core, chip] = jnp.concatenate([dev, dev_cross], axis=1).astype(BF16)
        own = e.at[j, core, chip]
        each(nc, chip, lambda k, q: put(AG, j, own, own, s, q * 2 + core))
        square = jnp.sum((dev * dev).reshape(piece // 8, 8, GROUP), axis=0) * 0.25
        double = jnp.sum((dev_cross * dev_cross).reshape(piece // 8, 8, HALF), axis=0) * 0.5
        off = mu - mean_ref[:, cols]
        off = off * off
        off = sum(off[:, i * HALF:(i + 1) * HALF] for i in range(BLOCK // HALF))
        head = (lax.broadcasted_iota(jnp.int32, (8, HALF), 0) + b == 0).astype(F32)
        tile = square[:, :HALF] + square[:, HALF:] + double + head * off
        if j == 0:
            lossb[0] = tile
        else:
            lossb[0] = lossb[0] + tile
        if j == nj - 1:
            each(nb, b, lambda k, q: put(LB, 0, lossb.at[0], lossb.at[nb - k], s, q))

    def swap(j):
        got(AG, j, e.at[j, core, pl.ds(1, nc - 1)])
        put(EX, j, e.at[j, core], e.at[j, core], s, mate)

    def pull(j):
        cols = slice(j * BLOCK, (j + 1) * BLOCK)
        mu = batch_mean(j)
        got(EX, j, e.at[j, 1 - core])
        c0 = (zall[s, j, :, :GROUP] - mu[:, :GROUP]).astype(BF16)
        c1 = (zall[s, j, :, GROUP:] - mu[:, GROUP:]).astype(BF16)
        e0, e1 = e[j, 0].reshape(GROUP, WIDE), e[j, 1].reshape(GROUP, WIDE)
        cross = jnp.concatenate([e0[:, GROUP:], e1[:, GROUP:]], axis=1)
        p0 = dot(c0, e0[:, :GROUP], ((1,), (0,))) + dot(c1, cross, ((1,), (1,)))
        p1 = dot(c0, cross, ((1,), (0,))) + dot(c1, e1[:, :GROUP], ((1,), (0,)))
        p = jnp.concatenate([p0, p1], axis=1) + 2.0 * (mu - mean_ref[:, cols])
        psend[j] = p.astype(BF16).reshape(nl, own_rows, BLOCK)
        each(nl, s, lambda k, q: put(PU, j, psend.at[j, q], pall.at[nl - k, j], q, b))
        pall[0, j] = psend[j, s]

    def slopes(j):
        cols = slice(j * BLOCK, (j + 1) * BLOCK)

        def layer(l, carry):
            at = slot(l)
            scale = ss[at, 0:1, cols]
            half = zall[l, j, pl.ds(pl.multiple_of(s * own_rows, own_rows), own_rows), :] * scale + ss[at, 1:2, cols]
            t = jnp.tanh(half)
            slope[l, j] = (1.0 + t) * (1.0 + half * (1.0 - t)) * scale
            return carry
        loop(nl, layer, 0)

    def backward(j):
        cols = slice(j * BLOCK, (j + 1) * BLOCK)

        got(PU, j, pall.at[pl.ds(1, nl - 1), j])

        def layer(i, up):
            l = nl - 1 - i
            at = slot(l)
            grad = (up * slope[l, j] + pall[at, j].astype(F32)).astype(BF16)
            w = wall[at, j].reshape(BLOCK, GROUP)
            parts = []
            for g in range(BLOCK // GROUP):
                part = slice(g * GROUP, (g + 1) * GROUP)
                parts.append(dot(grad[:, part], w[part], ((1,), (1,))))
            return jnp.concatenate(parts, axis=1).astype(BF16).astype(F32)
        up = loop(nl, layer, jnp.zeros((own_rows, BLOCK), F32))
        out_ref[:, cols] = up.astype(BF16)

    def loss_plane():
        got(LB, 0, lossb.at[pl.ds(1, nb - 1)])
        lossz[0] = jnp.sum(lossb[...], axis=0)
        each(nl, s, lambda k, q: put(LZ, 0, lossz.at[0], lossz.at[nl - k], q, b))

    def loss_all():
        got(LZ, 0, lossz.at[pl.ds(1, nl - 1)])
        loss_ref[0, 0] = jnp.sum(jnp.sum(lossz[...], axis=0)) * (1.0 / (nl * nj * BLOCK))

    def early_sends():
        sent(SS, ss.at[pl.ds(1, nl - 1)])
        sent(WZ, wall.at[pl.ds(1, nl - 1), :, chip, core])
        sent(WC, wall.at[pl.ds(1, nl - 1), :, pl.ds(1, nc - 1), core])
        sent(WM, wall.at[pl.ds(1, nl - 1), :, :, core])
        sent(ZC, zc.at[:, core])
        sent(MM, mub.at[:, chip, core])
        sent(MC, mub.at[:, pl.ds(1, nc - 1)])
        sent(RS, srs.at[:, pl.ds(1, nc - 1)])
        sent(AG, e.at[:, core, pl.ds(1, nc - 1)])
        sent(EX, e.at[:, core])

    Z, M, F, C, E, X, Q, S, B = (
        spread_chips, spread_mate, forward, gram, reduce, swap, pull, slopes, backward)
    order = [(Z, 0), (Z, 1), (Z, 2), (M, 0), (F, 0), (M, 1), (C, 0), (F, 1), (M, 2), (C, 1), (F, 2), (E, 0),
             (C, 2), (X, 0), (E, 1), (Q, 0), (X, 1), (E, 2), (Q, 1), (S, 0), (S, 1), (S, 2), (B, 0), (X, 2), (Q, 2)]
    for stage, j in order:
        stage(j)
    loss_plane()
    early_sends()
    for j in range(1, nj):
        backward(j)
    loss_all()
    sent(LZ, lossz.at[pl.ds(1, nl - 1)])
    sent(LB, lossb.at[pl.ds(1, nb - 1)])
    sent(PU, psend.at[:, pl.ds(1, nl - 1)])


def shards(nl, nb, images, weights, bn_mean, bn_var, bn_gain, bn_bias):
    rows, channels = images.shape[1:]
    nj = channels // BLOCK
    nc = nb // 2
    own_rows = rows // nl
    piece = GROUP // nc
    vmem, dma = pltpu.VMEM, pltpu.SemaphoreType.DMA
    halves = BLOCK // GROUP
    out, loss = pl.pallas_call(
        functools.partial(kernel, nl, nb, nj),
        out_shape=(jax.ShapeDtypeStruct((own_rows, channels), BF16),
                   jax.ShapeDtypeStruct((1, 1), F32)),
        in_specs=[pl.BlockSpec(memory_space=vmem)] * 6,
        out_specs=(pl.BlockSpec(memory_space=vmem), pl.BlockSpec(memory_space=pltpu.SMEM)),
        scratch_shapes=[
            vmem((nl, nj, nc, 2, BLOCK // nb, GROUP), BF16),
            vmem((nl, 2, channels), F32),
            vmem((rows, BLOCK), BF16),
            vmem((nl, nj, rows, BLOCK), F32),
            vmem((nl, nj, own_rows, BLOCK), F32),
            vmem((nj, 2, halves, rows, GROUP), BF16),
            vmem((nj, nc, piece, WIDE), F32),
            vmem((nj, nc, piece, WIDE), BF16),
            vmem((nj, nc, piece, WIDE), BF16),
            vmem((nj, 2, nc, piece, WIDE), BF16),
            vmem((nj, nl, own_rows, BLOCK), BF16),
            vmem((nl, nj, own_rows, BLOCK), BF16),
            vmem((nj, nc, 2, 1, BLOCK), F32),
            vmem((1, BLOCK), F32),
            vmem((nb, 8, 128), F32),
            vmem((nl, 8, 128), F32),
            dma((13,)),
            dma((13, nj)),
        ],
        compiler_params=pltpu.CompilerParams(
            collective_id=0, has_side_effects=True, vmem_limit_bytes=60 * 1024 * 1024),
    )(images[0], weights.reshape(nj, nc, 2, BLOCK // nb, GROUP), bn_mean, bn_var, bn_gain, bn_bias)
    return (out[None], loss.reshape(()))


def solution(mesh):
    placed = (
        P("batch", None, None),
        P("section", None, None, None),
        P("section", None),
        P("section", None),
        P("section", None),
        P("section", None),
    )
    return jax.shard_map(
        functools.partial(shards, mesh.shape["section"], mesh.shape["batch"]),
        mesh=mesh,
        in_specs=placed,
        out_specs=(P("batch", "section", None), P()),
        check_vma=False,
    )
```

time: 70.9 us -> 62.8 us (0.89)
  Pallas kernels: 66.7 us -> 58.6 us
    pallas_call x1, Pallas kernels: 66.7 us -> 58.6 us  [shards(): pl.pallas_call(functools.partial(kernel, nl, nb, nj), out_shape=(jax.Shap...]
where the time goes in v3:
time: 62.8 us; the launch traced here: 62.6 us
  Pallas kernels  58.6 us (93%)
  between operations  2.4 us (4%)
  local copies, waits for them, and re-layouts  1.62 us (3%)
    pallas_call x1, Pallas kernels, shards(): pl.pallas_call(functools.partial(kernel, nl, nb, nj), out_shape=(jax.Shap...  58.6 us
    unnamed x1, local copies, waits for them, and re-layouts  1.62 us

profile of v3, /device:TPU:0, one launch (start us, length us, event | category | flops | bytes accessed | tf_op | source)
XLA Modules:
  0.0 62.6 jit_solution(6288190044550904140)
XLA Ops:
  0.6 58.6 %shard_map.77 = (bf16[64,1536]{1,0:T(8,128)(2,1)}, f32[1,1]{1,0:T(1,128)}) custom-call(bf16[256,1536]{1,0:T(8,128)(2,1)} %bitcast.4, bf16[3,4,2,64,256]{4,3,2,1,0:T(8,128)(2,1)} %bitcast.5, f32[1,1536]{1,0:T(1,128)} %mean_ref.1, f32[1,1536]{1,0:T(1,128)} %var_ref.1, f32[1,1536]{1,0:T(1,128)} %gain_ref.1, f32[1,1536]{1,0:T(1,128)} %bias_ref.1), custom_call_target="tpu_custom_call" | custom-call | tf_op jit(solution)/shard_map/pallas_call | solution.py:279
  59.2 1.6 %copy.10 = bf16[1,64,1536]{2,1,0:T(8,128)(2,1)} copy(bf16[1,64,1536]{2,1,0:T(8,128)(2,1)} %bitcast.6) | data formatting | bytes 393216

commit v4 on v3

v4 whole, which is shorter than its diff:
```python
import functools

import jax
import jax.numpy as jnp
from jax import lax
from jax.experimental import pallas as pl
from jax.experimental.pallas import tpu as pltpu
from jax.sharding import PartitionSpec as P

BLOCK = 512
GROUP = 256
HALF = 128
WIDE = GROUP + HALF
EPS = 1e-05
MESH = pl.DeviceIdType.MESH
F32 = jnp.float32
BF16 = jnp.bfloat16


def dot(a, b, dims):
    return lax.dot_general(a, b, (dims, ((), ())), preferred_element_type=F32)


def kernel(nl, nb, nj, x_ref, w_ref, mean_ref, var_ref, gain_ref, bias_ref, out_ref, loss_ref,
           wall, pp, ppo, xbuf, zall, slope, zc, sacc, srs, rs, e, pall, gout, outv, mub, mu_all, lossb, lossz, lossw,
           send, recv):
    s = lax.axis_index("section")
    b = lax.axis_index("batch")
    chip, core = b // 2, b % 2
    nc = nb // 2
    mate = chip * 2 + (1 - core)
    rows = x_ref.shape[0]
    own_rows = rows // nl
    piece = GROUP // nc
    row_total = rows * nb

    def copy(src, dst, ssem, rsem, sec, bat):
        return pltpu.make_async_remote_copy(
            src_ref=src, dst_ref=dst, send_sem=ssem, recv_sem=rsem,
            device_id=(sec, bat), device_id_type=MESH)

    def each(count, me, body):
        if count <= 8:
            for k in range(1, count):
                body(k, lax.rem(me + k, count))
        else:
            def step(k, carry):
                body(k, lax.rem(me + k, count))
                return carry
            lax.fori_loop(1, count, step, 0)

    def loop(count, body, carry):
        if count > 8:
            return lax.fori_loop(0, count, body, carry)
        for i in range(count):
            carry = body(i, carry)
        return carry

    def slot(l):
        return lax.rem(l - s + nl, nl)

    WZ, PP, WC, WM, ZC, MM, MC, RS, AG, EX, GO, LB, LZ = range(13)
    block = jnp.minimum(s, nj - 1)

    def got(kind, j, ref):
        copy(ref, ref, send.at[kind, 0], recv.at[kind, j], s, mate).wait_recv()

    def sent(kind, ref, j=0):
        copy(ref, ref, send.at[kind, j], recv.at[kind, 0], s, mate).wait_send()

    def put(kind, j, src, dst, sec, bat, out=0):
        copy(src, dst, send.at[kind, out], recv.at[kind, j], sec, bat).start()

    def planes(body):
        for j in range(nj):
            pl.when(j != s)(functools.partial(body, j))

    barrier = pltpu.get_barrier_semaphore()
    each(nb, b, lambda k, q: pl.semaphore_signal(barrier, inc=1, device_id=(s, q), device_id_type=MESH))
    each(nl, s, lambda k, q: pl.semaphore_signal(barrier, inc=1, device_id=(q, b), device_id_type=MESH))
    scale_own = gain_ref[...] * lax.rsqrt(var_ref[...] + EPS)
    shift_own = bias_ref[...] - mean_ref[...] * scale_own
    for j in range(nj):
        cols = slice(j * BLOCK, (j + 1) * BLOCK)
        ppo[j, 0:1, :] = 0.5 * scale_own[:, cols]
        ppo[j, 1:2, :] = 0.5 * shift_own[:, cols]
        ppo[j, 2:3, :] = mean_ref[:, cols]
        ppo[j, 3:4, :] = var_ref[:, cols]
    pp[0] = ppo[block]
    wall[0] = w_ref[block]
    pl.semaphore_wait(barrier, nb - 1 + nl - 1)

    def send_layer(j):
        at = lax.rem(s - j + nl, nl)
        put(WZ, 0, w_ref.at[j, chip, core], wall.at[at, chip, core], j, b, j)
        put(PP, 0, ppo.at[j], pp.at[at], j, b, j)
    planes(send_layer)

    def gather_weights():
        mine = wall.at[pl.ds(1, nl - 1), chip, core]
        got(WZ, 0, mine)
        each(nc, chip, lambda k, q: put(WC, 0, mine, mine, s, q * 2 + core))
        got(PP, 0, pp.at[pl.ds(1, nl - 1)])
        xbuf[...] = x_ref[:, pl.ds(pl.multiple_of(block * BLOCK, BLOCK), BLOCK)]
        got(WC, 0, wall.at[pl.ds(1, nl - 1), pl.ds(1, nc - 1), core])
        mine = wall.at[pl.ds(1, nl - 1), :, core]
        put(WM, 0, mine, mine, s, mate)
        got(WM, 0, wall.at[pl.ds(1, nl - 1), :, 1 - core])

    def forward(j):
        at = slot(j)
        w = wall[at].reshape(BLOCK, GROUP)
        for g in range(BLOCK // GROUP):
            part = slice(g * GROUP, (g + 1) * GROUP)
            z = dot(xbuf[:, part], w[part], ((1,), (0,)))
            zall[j, :, part] = z
            half = z * pp[at, 0:1, part] + pp[at, 1:2, part]
            xbuf[:, part] = (half + half * jnp.tanh(half)).astype(BF16)
        z = zall[j]
        mu = jnp.sum(z, axis=0, keepdims=True) * (1.0 / rows)
        mub[j, chip, core] = mu
        put(MM, j, mub.at[j, chip, core], mub.at[j, chip, core], s, mate)
        centered = (z - mu).astype(BF16)
        for h in range(BLOCK // GROUP):
            zc[j, core, h] = centered[:, h * GROUP:(h + 1) * GROUP]
        put(ZC, j, zc.at[j, core], zc.at[j, core], s, mate)

    def gram(j):
        got(MM, j, mub.at[j, chip, 1 - core])
        each(nc, chip, lambda k, q: put(MC, j, mub.at[j, chip], mub.at[j, chip], s, q * 2 + core))
        got(ZC, j, zc.at[j, 1 - core])
        cross = pl.ds(pl.multiple_of(core * HALF, HALF), HALF)
        square = dot(zc[j, 0, core], zc[j, 0, core], ((0,), (0,))) + dot(
            zc[j, 1, core], zc[j, 1, core], ((0,), (0,)))
        other = dot(zc[j, 0, 0], zc[j, 0, 1, :, cross], ((0,), (0,))) + dot(
            zc[j, 1, 0], zc[j, 1, 1, :, cross], ((0,), (0,)))
        total = jnp.concatenate([square, other], axis=1).reshape(nc, piece, WIDE)
        sacc[j] = total
        srs[j] = total.astype(BF16)
        each(nc, chip, lambda k, q: put(RS, j, srs.at[j, q], rs.at[j, nc - k], s, q * 2 + core))

    def batch_mean(j):
        return jnp.sum(mub[j], axis=(0, 1)) * (1.0 / nb)

    def reduce(j):
        at = slot(j)
        got(MC, j, mub.at[j, pl.ds(1, nc - 1)])
        mu = batch_mean(j)
        mine = pl.ds(pl.multiple_of(core * GROUP, GROUP), GROUP)
        cross = pl.ds(pl.multiple_of(GROUP + core * HALF, HALF), HALF)
        mu_all[...] = mu
        mu_mine, mu_cross, mu_low = mu_all[:, mine], mu_all[:, cross], mu[:, :GROUP]
        eye = (lax.broadcasted_iota(jnp.int32, (piece, GROUP), 0) + chip * piece
               == lax.broadcasted_iota(jnp.int32, (piece, GROUP), 1)).astype(F32)

        def between(i, acc):
            low = mub[j, i // 2, i % 2, :, :GROUP] - mu_low
            d_mine = mub[j, i // 2, i % 2, :, mine] - mu_mine
            d_cross = mub[j, i // 2, i % 2, :, cross] - mu_cross
            column = jnp.sum(eye * d_mine, axis=1, keepdims=True)
            column_low = jnp.sum(eye * low, axis=1, keepdims=True)
            return (acc[0] + column * d_mine, acc[1] + column_low * d_cross)
        corr = jnp.concatenate(loop(
            nb, between, (jnp.zeros((piece, GROUP), F32), jnp.zeros((piece, HALF), F32))), axis=1)
        cov = sacc[j, chip] + corr * rows
        got(RS, j, rs.at[j, pl.ds(1, nc - 1)])
        cov = loop(nc - 1, lambda i, acc: acc + rs[j, i + 1].astype(F32), cov) * (1.0 / row_total)
        dev, dev_cross = cov[:, :GROUP] - eye * pp[at, 3:4, mine], cov[:, GROUP:]
        e[j, core, chip] = jnp.concatenate([dev, dev_cross], axis=1).astype(BF16)
        own = e.at[j, core, chip]
        each(nc, chip, lambda k, q: put(AG, j, own, own, s, q * 2 + core))
        square = jnp.sum((dev * dev).reshape(piece // 8, 8, GROUP), axis=0) * 0.25
        double = jnp.sum((dev_cross * dev_cross).reshape(piece // 8, 8, HALF), axis=0) * 0.5
        off = mu - pp[at, 2:3, :]
        off = off * off
        off = sum(off[:, i * HALF:(i + 1) * HALF] for i in range(BLOCK // HALF))
        head = (lax.broadcasted_iota(jnp.int32, (8, HALF), 0) + b == 0).astype(F32)
        tile = square[:, :HALF] + square[:, HALF:] + double + head * off
        lossb[b] = tile if j == 0 else lossb[b] + tile
        if j == nl - 1:
            each(nb, b, lambda k, q: put(LB, 0, lossb.at[b], lossb.at[b], s, q))

    def swap(j):
        got(AG, j, e.at[j, core, pl.ds(1, nc - 1)])
        put(EX, j, e.at[j, core], e.at[j, core], s, mate)

    def pull(j):
        mu = batch_mean(j)
        got(EX, j, e.at[j, 1 - core])
        c0 = (zall[j, :, :GROUP] - mu[:, :GROUP]).astype(BF16)
        c1 = (zall[j, :, GROUP:] - mu[:, GROUP:]).astype(BF16)
        e0, e1 = e[j, 0].reshape(GROUP, WIDE), e[j, 1].reshape(GROUP, WIDE)
        cross = jnp.concatenate([e0[:, GROUP:], e1[:, GROUP:]], axis=1)
        p0 = dot(c0, e0[:, :GROUP], ((1,), (0,))) + dot(c1, cross, ((1,), (1,)))
        p1 = dot(c0, cross, ((1,), (0,))) + dot(c1, e1[:, :GROUP], ((1,), (0,)))
        p = jnp.concatenate([p0, p1], axis=1) + 2.0 * (mu - pp[slot(j), 2:3, :])
        pall[j] = p.astype(BF16)

    def slopes(j):
        at = slot(j)
        scale = pp[at, 0:1, :]
        half = zall[j] * scale + pp[at, 1:2, :]
        t = jnp.tanh(half)
        slope[j] = (1.0 + t) * (1.0 + half * (1.0 - t)) * scale

    def backward():
        for g in range(BLOCK // GROUP):
            part = slice(g * GROUP, (g + 1) * GROUP)

            def layer(i, up):
                l = nl - 1 - i
                w = wall[slot(l)].reshape(BLOCK, GROUP)[part]
                grad = (up * slope[l, :, part] + pall[l, :, part].astype(F32)).astype(BF16)
                return dot(grad, w, ((1,), (1,))).astype(BF16).astype(F32)
            up = loop(nl, layer, jnp.zeros((rows, GROUP), F32))
            gout[:, :, part] = up.astype(BF16).reshape(nl, own_rows, GROUP)
        each(nl, s, lambda k, q: put(GO, block, gout.at[q], outv.at[block], q, b))
        outv[block] = gout[s]

    def loss_plane():
        got(LB, 0, lossb.at[pl.ds(1, nb - 1)])
        lossz[block] = jnp.sum(lossb[...], axis=0)
        each(nl, s, lambda k, q: put(LZ, block, lossz.at[block], lossz.at[block], q, b))

    def early_sends():
        sent(WC, wall.at[pl.ds(1, nl - 1), pl.ds(1, nc - 1), core])
        sent(WM, wall.at[pl.ds(1, nl - 1), :, core])
        sent(ZC, zc.at[:, core])
        sent(MM, mub.at[:, chip, core])
        sent(MC, mub.at[:, pl.ds(1, nc - 1)])
        sent(RS, srs.at[:, pl.ds(1, nc - 1)])
        sent(AG, e.at[:, core, pl.ds(1, nc - 1)])
        sent(EX, e.at[:, core])
        sent(LB, lossb.at[pl.ds(1, nb - 1)])

    @pl.when(s < nj)
    def _():
        gather_weights()
        last = nl - 1
        for t in range(nl + 4):
            for stage, delay in ((forward, 0), (gram, 1), (reduce, 3), (swap, 4), (pull, 5)):
                l = t - delay
                if 0 <= l < nl and not (stage is swap and l == last) and not (stage is pull and l >= last):
                    stage(l)
        for l in range(nl):
            slopes(l)
        swap(last)
        loss_plane()
        pull(last)
        backward()
        early_sends()
        sent(GO, gout.at[pl.ds(1, nl - 1)])
        sent(LZ, lossw.at[pl.ds(1, nl - 1)])

    def sent_layer(j):
        sent(WZ, w_ref.at[j, chip, core], j)
        sent(PP, ppo.at[j], j)
    planes(sent_layer)

    def arrived(j):
        got(LZ, j, lossz.at[j])
        got(GO, j, outv.at[j])
    planes(arrived)
    loss_ref[0, 0] = jnp.sum(jnp.sum(lossz[...], axis=0)) * (1.0 / (nl * nj * BLOCK))
    for j in range(nj):
        out_ref[:, j * BLOCK:(j + 1) * BLOCK] = outv[j]


def shards(nl, nb, images, weights, bn_mean, bn_var, bn_gain, bn_bias):
    rows, channels = images.shape[1:]
    nj = channels // BLOCK
    nc = nb // 2
    own_rows = rows // nl
    piece = GROUP // nc
    vmem, dma = pltpu.VMEM, pltpu.SemaphoreType.DMA
    halves = BLOCK // GROUP
    out, loss = pl.pallas_call(
        functools.partial(kernel, nl, nb, nj),
        out_shape=(jax.ShapeDtypeStruct((own_rows, channels), BF16),
                   jax.ShapeDtypeStruct((1, 1), F32)),
        in_specs=[pl.BlockSpec(memory_space=vmem)] * 6,
        out_specs=(pl.BlockSpec(memory_space=vmem), pl.BlockSpec(memory_space=pltpu.SMEM)),
        scratch_shapes=[
            vmem((nl, nc, 2, BLOCK // nb, GROUP), BF16),
            vmem((nl, 4, BLOCK), F32),
            vmem((nj, 4, BLOCK), F32),
            vmem((rows, BLOCK), BF16),
            vmem((nl, rows, BLOCK), F32),
            vmem((nl, rows, BLOCK), F32),
            vmem((nl, 2, halves, rows, GROUP), BF16),
            vmem((nl, nc, piece, WIDE), F32),
            vmem((nl, nc, piece, WIDE), BF16),
            vmem((nl, nc, piece, WIDE), BF16),
            vmem((nl, 2, nc, piece, WIDE), BF16),
            vmem((nl, rows, BLOCK), BF16),
            vmem((nl, own_rows, BLOCK), BF16),
            vmem((nj, own_rows, BLOCK), BF16),
            vmem((nl, nc, 2, 1, BLOCK), F32),
            vmem((1, BLOCK), F32),
            vmem((nb, 8, 128), F32),
            vmem((nj, 8, 128), F32),
            vmem((nl, 8, 128), F32),
            dma((13, nj)),
            dma((13, nl)),
        ],
        compiler_params=pltpu.CompilerParams(
            collective_id=0, has_side_effects=True, vmem_limit_bytes=60 * 1024 * 1024),
    )(images[0], weights.reshape(nj, nc, 2, BLOCK // nb, GROUP), bn_mean, bn_var, bn_gain, bn_bias)
    return (out[None], loss.reshape(()))


def solution(mesh):
    placed = (
        P("batch", None, None),
        P("section", None, None, None),
        P("section", None),
        P("section", None),
        P("section", None),
        P("section", None),
    )
    return jax.shard_map(
        functools.partial(shards, mesh.shape["section"], mesh.shape["batch"]),
        mesh=mesh,
        in_specs=placed,
        out_specs=(P("batch", "section", None), P()),
        check_vma=False,
    )
```

time: 62.8 us -> 53.6 us (0.85)
  Pallas kernels: 58.6 us -> 49 us
    pallas_call x1, Pallas kernels: 58.6 us -> 49 us  [shards(): pl.pallas_call(functools.partial(kernel, nl, nb, nj), out_shape=(jax.Shap...]
where the time goes in v4:
time: 53.6 us; the launch traced here: 53 us
  Pallas kernels  49 us (91%)
  between operations  2.4 us (4%)
  local copies, waits for them, and re-layouts  1.62 us (3%)
    pallas_call x1, Pallas kernels, shards(): pl.pallas_call(functools.partial(kernel, nl, nb, nj), out_shape=(jax.Shap...  49 us
    unnamed x1, local copies, waits for them, and re-layouts  1.62 us

profile of v4, /device:TPU:0, one launch (start us, length us, event | category | flops | bytes accessed | tf_op | source)
XLA Modules:
  0.0 53.0 jit_solution(8474489704945838250)
XLA Ops:
  0.6 49.0 %shard_map.77 = (bf16[64,1536]{1,0:T(8,128)(2,1)}, f32[1,1]{1,0:T(1,128)}) custom-call(bf16[256,1536]{1,0:T(8,128)(2,1)} %bitcast.4, bf16[3,4,2,64,256]{4,3,2,1,0:T(8,128)(2,1)} %bitcast.5, f32[1,1536]{1,0:T(1,128)} %mean_ref.1, f32[1,1536]{1,0:T(1,128)} %var_ref.1, f32[1,1536]{1,0:T(1,128)} %gain_ref.1, f32[1,1536]{1,0:T(1,128)} %bias_ref.1), custom_call_target="tpu_custom_call" | custom-call | tf_op jit(solution)/shard_map/pallas_call | solution.py:277
  49.6 1.6 %copy.10 = bf16[1,64,1536]{2,1,0:T(8,128)(2,1)} copy(bf16[1,64,1536]{2,1,0:T(8,128)(2,1)} %bitcast.6) | data formatting | bytes 393216

commit v5 on v4

--- a/solution.py
+++ b/solution.py
@@ -92,23 +92,30 @@
 
     def send_layer(j):
         at = lax.rem(s - j + nl, nl)
-        put(WZ, 0, w_ref.at[j, chip, core], wall.at[at, chip, core], j, b, j)
-        put(PP, 0, ppo.at[j], pp.at[at], j, b, j)
+        put(WZ, s, w_ref.at[j, chip, core], wall.at[at, chip, core], j, b, j)
+        put(PP, s, ppo.at[j], pp.at[at], j, b, j)
     planes(send_layer)
 
-    def gather_weights():
-        mine = wall.at[pl.ds(1, nl - 1), chip, core]
-        got(WZ, 0, mine)
-        each(nc, chip, lambda k, q: put(WC, 0, mine, mine, s, q * 2 + core))
-        got(PP, 0, pp.at[pl.ds(1, nl - 1)])
-        xbuf[...] = x_ref[:, pl.ds(pl.multiple_of(block * BLOCK, BLOCK), BLOCK)]
-        got(WC, 0, wall.at[pl.ds(1, nl - 1), pl.ds(1, nc - 1), core])
-        mine = wall.at[pl.ds(1, nl - 1), :, core]
-        put(WM, 0, mine, mine, s, mate)
-        got(WM, 0, wall.at[pl.ds(1, nl - 1), :, 1 - core])
+    def others(stage):
+        return lambda l: pl.when(l != s)(functools.partial(stage, l))
+
+    def spread_chips(l):
+        mine = wall.at[slot(l), chip, core]
+        got(WZ, l, mine)
+        each(nc, chip, lambda k, q: put(WC, l, mine, mine, s, q * 2 + core))
+
+    def spread_mate(l):
+        got(WC, l, wall.at[slot(l), pl.ds(1, nc - 1), core])
+        mine = wall.at[slot(l), :, core]
+        put(WM, l, mine, mine, s, mate)
+
+    def weights_here(l):
+        got(WM, l, wall.at[slot(l), :, 1 - core])
+        got(PP, l, pp.at[slot(l)])
 
     def forward(j):
         at = slot(j)
+        others(weights_here)(j)
         w = wall[at].reshape(BLOCK, GROUP)
         for g in range(BLOCK // GROUP):
             part = slice(g * GROUP, (g + 1) * GROUP)
@@ -213,9 +220,10 @@
                 grad = (up * slope[l, :, part] + pall[l, :, part].astype(F32)).astype(BF16)
                 return dot(grad, w, ((1,), (1,))).astype(BF16).astype(F32)
             up = loop(nl, layer, jnp.zeros((rows, GROUP), F32))
-            gout[:, :, part] = up.astype(BF16).reshape(nl, own_rows, GROUP)
-        each(nl, s, lambda k, q: put(GO, block, gout.at[q], outv.at[block], q, b))
-        outv[block] = gout[s]
+            gout[g] = up.astype(BF16).reshape(nl, own_rows, GROUP)
+            each(nl, s, lambda k, q: put(GO, g * nl + block, gout.at[g, q], outv.at[block, g], q, b))
+        for g in range(BLOCK // GROUP):
+            outv[block, g] = gout[g, s]
 
     def loss_plane():
         got(LB, 0, lossb.at[pl.ds(1, nb - 1)])
@@ -235,10 +243,12 @@
 
     @pl.when(s < nj)
     def _():
-        gather_weights()
+        xbuf[...] = x_ref[:, pl.ds(pl.multiple_of(block * BLOCK, BLOCK), BLOCK)]
+        for l in range(nl):
+            others(spread_chips)(l)
         last = nl - 1
-        for t in range(nl + 4):
-            for stage, delay in ((forward, 0), (gram, 1), (reduce, 3), (swap, 4), (pull, 5)):
+        for t in range(nl + 5):
+            for stage, delay in ((others(spread_mate), 0), (forward, 1), (gram, 2), (reduce, 4), (swap, 5), (pull, 6)):
                 l = t - delay
                 if 0 <= l < nl and not (stage is swap and l == last) and not (stage is pull and l >= last):
                     stage(l)
@@ -249,7 +259,7 @@
         pull(last)
         backward()
         early_sends()
-        sent(GO, gout.at[pl.ds(1, nl - 1)])
+        sent(GO, gout.at[:, pl.ds(1, nl - 1)])
         sent(LZ, lossw.at[pl.ds(1, nl - 1)])
 
     def sent_layer(j):
@@ -259,11 +269,13 @@
 
     def arrived(j):
         got(LZ, j, lossz.at[j])
-        got(GO, j, outv.at[j])
+        for g in range(BLOCK // GROUP):
+            got(GO, g * nl + j, outv.at[j, g])
     planes(arrived)
     loss_ref[0, 0] = jnp.sum(jnp.sum(lossz[...], axis=0)) * (1.0 / (nl * nj * BLOCK))
     for j in range(nj):
-        out_ref[:, j * BLOCK:(j + 1) * BLOCK] = outv[j]
+        for g in range(BLOCK // GROUP):
+            out_ref[:, j * BLOCK + g * GROUP:j * BLOCK + (g + 1) * GROUP] = outv[j, g]
 
 
 def shards(nl, nb, images, weights, bn_mean, bn_var, bn_gain, bn_bias):
@@ -293,15 +305,15 @@
             vmem((nl, nc, piece, WIDE), BF16),
             vmem((nl, 2, nc, piece, WIDE), BF16),
             vmem((nl, rows, BLOCK), BF16),
-            vmem((nl, own_rows, BLOCK), BF16),
-            vmem((nj, own_rows, BLOCK), BF16),
+            vmem((halves, nl, own_rows, GROUP), BF16),
+            vmem((nj, halves, own_rows, GROUP), BF16),
             vmem((nl, nc, 2, 1, BLOCK), F32),
             vmem((1, BLOCK), F32),
             vmem((nb, 8, 128), F32),
             vmem((nj, 8, 128), F32),
             vmem((nl, 8, 128), F32),
             dma((13, nj)),
-            dma((13, nl)),
+            dma((13, 2 * nl)),
         ],
         compiler_params=pltpu.CompilerParams(
             collective_id=0, has_side_effects=True, vmem_limit_bytes=60 * 1024 * 1024),

time: 53.6 us -> 50.7 us (0.946)
  Pallas kernels: 49 us -> 46.5 us
    pallas_call x1, Pallas kernels: 49 us -> 46.5 us  [shards(): pl.pallas_call(functools.partial(kernel, nl, nb, nj), out_shape=(jax.Shap...]
where the time goes in v5:
time: 50.7 us; the launch traced here: 50.5 us
  Pallas kernels  46.5 us (92%)
  between operations  2.4 us (5%)
  local copies, waits for them, and re-layouts  1.62 us (3%)
    pallas_call x1, Pallas kernels, shards(): pl.pallas_call(functools.partial(kernel, nl, nb, nj), out_shape=(jax.Shap...  46.5 us
    unnamed x1, local copies, waits for them, and re-layouts  1.62 us

profile of v5, /device:TPU:0, one launch (start us, length us, event | category | flops | bytes accessed | tf_op | source)
XLA Modules:
  0.0 50.5 jit_solution(8190446553520754020)
XLA Ops:
  0.6 46.5 %shard_map.77 = (bf16[64,1536]{1,0:T(8,128)(2,1)}, f32[1,1]{1,0:T(1,128)}) custom-call(bf16[256,1536]{1,0:T(8,128)(2,1)} %bitcast.4, bf16[3,4,2,64,256]{4,3,2,1,0:T(8,128)(2,1)} %bitcast.5, f32[1,1536]{1,0:T(1,128)} %mean_ref.1, f32[1,1536]{1,0:T(1,128)} %var_ref.1, f32[1,1536]{1,0:T(1,128)} %gain_ref.1, f32[1,1536]{1,0:T(1,128)} %bias_ref.1), custom_call_target="tpu_custom_call" | custom-call | tf_op jit(solution)/shard_map/pallas_call | solution.py:289
  47.1 1.6 %copy.10 = bf16[1,64,1536]{2,1,0:T(8,128)(2,1)} copy(bf16[1,64,1536]{2,1,0:T(8,128)(2,1)} %bitcast.6) | data formatting | bytes 393216

commit v6 on v5

--- a/solution.py
+++ b/solution.py
@@ -247,13 +247,11 @@
         for l in range(nl):
             others(spread_chips)(l)
         last = nl - 1
-        for t in range(nl + 5):
-            for stage, delay in ((others(spread_mate), 0), (forward, 1), (gram, 2), (reduce, 4), (swap, 5), (pull, 6)):
+        for t in range(nl + 7):
+            for stage, delay in ((others(spread_mate), 0), (forward, 1), (gram, 2), (reduce, 4), (slopes, 5), (swap, 7), (pull, 8)):
                 l = t - delay
                 if 0 <= l < nl and not (stage is swap and l == last) and not (stage is pull and l >= last):
                     stage(l)
-        for l in range(nl):
-            slopes(l)
         swap(last)
         loss_plane()
         pull(last)

time: 50.7 us -> 50.3 us (level)
  no operation moved by 1% of the time
where the time goes in v6:
time: 50.3 us; the launch traced here: 50.1 us
  Pallas kernels  46.1 us (92%)
  between operations  2.4 us (5%)
  local copies, waits for them, and re-layouts  1.62 us (3%)
    pallas_call x1, Pallas kernels, shards(): pl.pallas_call(functools.partial(kernel, nl, nb, nj), out_shape=(jax.Shap...  46.1 us
    unnamed x1, local copies, waits for them, and re-layouts  1.62 us

profile of v6, /device:TPU:0, one launch (start us, length us, event | category | flops | bytes accessed | tf_op | source)
XLA Modules:
  0.0 50.1 jit_solution(11026710205834544460)
XLA Ops:
  0.6 46.1 %shard_map.77 = (bf16[64,1536]{1,0:T(8,128)(2,1)}, f32[1,1]{1,0:T(1,128)}) custom-call(bf16[256,1536]{1,0:T(8,128)(2,1)} %bitcast.4, bf16[3,4,2,64,256]{4,3,2,1,0:T(8,128)(2,1)} %bitcast.5, f32[1,1536]{1,0:T(1,128)} %mean_ref.1, f32[1,1536]{1,0:T(1,128)} %var_ref.1, f32[1,1536]{1,0:T(1,128)} %gain_ref.1, f32[1,1536]{1,0:T(1,128)} %bias_ref.1), custom_call_target="tpu_custom_call" | custom-call | tf_op jit(solution)/shard_map/pallas_call | solution.py:287
  46.8 1.6 %copy.10 = bf16[1,64,1536]{2,1,0:T(8,128)(2,1)} copy(bf16[1,64,1536]{2,1,0:T(8,128)(2,1)} %bitcast.6) | data formatting | bytes 393216

commit v7 on v6

--- a/solution.py
+++ b/solution.py
@@ -248,7 +248,7 @@
             others(spread_chips)(l)
         last = nl - 1
         for t in range(nl + 7):
-            for stage, delay in ((others(spread_mate), 0), (forward, 1), (gram, 2), (reduce, 4), (slopes, 5), (swap, 7), (pull, 8)):
+            for stage, delay in ((others(spread_mate), 0), (forward, 1), (gram, 2), (reduce, 3), (slopes, 5), (swap, 7), (pull, 8)):
                 l = t - delay
                 if 0 <= l < nl and not (stage is swap and l == last) and not (stage is pull and l >= last):
                     stage(l)

time: 50.3 us -> 50.6 us (level)
  no operation moved by 1% of the time
where the time goes in v7:
time: 50.6 us; the launch traced here: 50.4 us
  Pallas kernels  46.4 us (92%)
  between operations  2.4 us (5%)
  local copies, waits for them, and re-layouts  1.62 us (3%)
    pallas_call x1, Pallas kernels, shards(): pl.pallas_call(functools.partial(kernel, nl, nb, nj), out_shape=(jax.Shap...  46.4 us
    unnamed x1, local copies, waits for them, and re-layouts  1.62 us

profile of v7, /device:TPU:0, one launch (start us, length us, event | category | flops | bytes accessed | tf_op | source)
XLA Modules:
  0.0 50.4 jit_solution(6307041850335830501)
XLA Ops:
  0.6 46.4 %shard_map.77 = (bf16[64,1536]{1,0:T(8,128)(2,1)}, f32[1,1]{1,0:T(1,128)}) custom-call(bf16[256,1536]{1,0:T(8,128)(2,1)} %bitcast.4, bf16[3,4,2,64,256]{4,3,2,1,0:T(8,128)(2,1)} %bitcast.5, f32[1,1536]{1,0:T(1,128)} %mean_ref.1, f32[1,1536]{1,0:T(1,128)} %var_ref.1, f32[1,1536]{1,0:T(1,128)} %gain_ref.1, f32[1,1536]{1,0:T(1,128)} %bias_ref.1), custom_call_target="tpu_custom_call" | custom-call | tf_op jit(solution)/shard_map/pallas_call | solution.py:287
  47.0 1.6 %copy.10 = bf16[1,64,1536]{2,1,0:T(8,128)(2,1)} copy(bf16[1,64,1536]{2,1,0:T(8,128)(2,1)} %bitcast.6) | data formatting | bytes 393216
